TPU v7x, 512 devices: a whole 4x8x8 slice. The times are simulated.
512 devices in a mesh: seq: 128 (over z, x_lo, y), batch: 4 (over x_hi, core).
Axes of the slice: x: 4 (x_hi: 2, x_lo: 2; x = x_hi * 2 + x_lo), y: 8, z: 8, core: 2. Of those that a mesh axis runs over, the one named last changes fastest.
Arguments:
- coarse_act: bfloat16 [8, 8192, 1536], P('batch', 'seq'), may hold values from -6 to 6
- skip_act: bfloat16 [8, 16384, 1536], P('batch', 'seq'), may hold values from -6 to 6
- proj_in: bfloat16 [1536, 1536], P('seq'), may hold values from -0.15625 to 0.15625
- proj_out: bfloat16 [1536, 1536], P('seq'), may hold values from -0.15625 to 0.15625
- depth_kernel: float32 [3, 1536], replicated, may hold values from -3.5 to 3.5
- norm_gain: float32 [1536], replicated, may hold values from 0.5 to 1.5
- grad_out: bfloat16 [8, 16384, 1536], P('batch', 'seq'), may hold values from -6 to 6
Outputs:
- block_out: bfloat16 [8, 16384, 1536], P('batch', 'seq')
- grad_coarse_act: bfloat16 [8, 8192, 1536], P('batch', 'seq')
- grad_kernel: float32 [3, 1536], replicated
- grad_gain: float32 [1536], replicated
All inputs are finite; a program needn't handle non-finite values.
Results may differ from a plain program's by a relative error of at most 0.012.
Values may be sent and summed in bfloat16 or wider, within the bound.
A program may use at most 128 MiB of HBM per device.

v0:
```python
import jax
import jax.numpy as jnp
from jax import lax
from jax.sharding import Mesh
from jax.sharding import PartitionSpec as P

SEQ = ("seq_0", "seq_1", "seq_2")
SEQ_BATCH = ("seq_0", "seq_1", "seq_2", "batch_0", "batch_1")
BATCH = ("batch_0", "batch_1")


epsilon = 1e-05


def joined_along(pieces, dim):
    pieces = jnp.moveaxis(pieces, 0, dim)
    shape = pieces.shape
    return pieces.reshape(*shape[:dim], shape[dim] * shape[dim + 1], *shape[dim + 2 :])


def all_blocks(x, axes, turns):
    pieces = x[None]
    for k in turns:
        pieces = lax.all_gather(pieces, axes[k], axis=0, tiled=True)
    current = [lax.axis_size(axes[k]) for k in reversed(turns)]
    pieces = pieces.reshape(*current, *x.shape)
    turned = sorted(range(len(turns)), key=lambda place: turns[len(turns) - 1 - place])
    return pieces.transpose(*turned, *range(len(turns), pieces.ndim)).reshape(-1, *x.shape)


def whole_of(x, axes, turns, dim):
    return joined_along(all_blocks(x, axes, turns), dim)


def with_halo(cells, sides, width):
    for axis, dim in sides:
        count = lax.axis_size(axis)
        ends = count - 1
        head = lax.slice_in_dim(cells, 0, width, axis=dim)
        tail = lax.slice_in_dim(cells, cells.shape[dim] - width, cells.shape[dim], axis=dim)
        cells = jnp.concatenate(
            [
                lax.ppermute(tail, axis, [(i, (i + 1) % count) for i in range(ends)]),
                cells,
                lax.ppermute(head, axis, [((i + 1) % count, i) for i in range(ends)]),
            ],
            axis=dim,
        )
    return cells


def by_axis(x, axes):
    for axis in axes:
        x = lax.psum(x, axis)
    return x


def norm_gelu(values_in, gain):
    values = values_in.astype(jnp.float32)
    average = jnp.mean(values, axis=-1, keepdims=True)
    centered = values - average
    variance = jnp.mean(centered * centered, axis=-1, keepdims=True)
    return jax.nn.gelu(centered * lax.rsqrt(variance + epsilon) * gain, approximate=False)


def fetch(weights):
    return whole_of(weights, SEQ, (1, 0, 2), 0)


def on_device(coarse_act, skip_act, proj_in, proj_out, depth_kernel, norm_gain, grad_out):
    whole_in = fetch(proj_in)
    activated = norm_gelu(coarse_act, norm_gain)
    act_low = activated.astype(jnp.bfloat16)
    whole_out = fetch(proj_out)
    coarse = jnp.einsum(
        "sbi,io->sbo", act_low, whole_in, preferred_element_type=jnp.float32
    ).astype(jnp.bfloat16)
    merged = (
        jnp.repeat(coarse, 2, axis=1).astype(jnp.float32) + skip_act.astype(jnp.float32)
    ).astype(jnp.bfloat16)
    padded = with_halo(merged, ((SEQ, 1),), 1)
    rows = merged.shape[1]
    mixed = (
        depth_kernel[0] * padded[:, :-2]
        + depth_kernel[1] * padded[:, 1:-1]
        + depth_kernel[2] * padded[:, 2:]
    )
    mixed = mixed.astype(jnp.bfloat16)
    block_out = jnp.einsum(
        "sbi,io->sbo", mixed, whole_out, preferred_element_type=jnp.float32
    ).astype(jnp.bfloat16)
    grad_mixed = jnp.einsum(
        "sbo,io->sbi", grad_out, whole_out, preferred_element_type=jnp.float32
    ).astype(jnp.bfloat16)
    grad_pad = with_halo(grad_mixed, ((SEQ, 1),), 1).astype(jnp.float32)
    grad_wide = grad_pad[:, 1:-1]
    kernel_part = jnp.stack(
        [
            jnp.sum(padded[:, shift : shift + rows].astype(jnp.float32) * grad_wide, axis=(0, 1))
            for shift in range(3)
        ]
    )
    grad_merged = (
        depth_kernel[0] * grad_pad[:, 2:]
        + depth_kernel[1] * grad_pad[:, 1:-1]
        + depth_kernel[2] * grad_pad[:, :-2]
    )
    grad_coarse = jnp.sum(
        grad_merged.reshape(grad_merged.shape[0], rows // 2, 2, grad_merged.shape[2]), axis=2
    ).astype(jnp.bfloat16)
    grad_act = jnp.einsum("sbo,io->sbi", grad_coarse, whole_in, preferred_element_type=jnp.float32)
    unused, pullback = jax.vjp(norm_gelu, coarse_act, norm_gain)
    grad_cur, gain_part = pullback(grad_act)
    grad_kernel, grad_gain = (by_axis(kernel_part, SEQ_BATCH), by_axis(gain_part, SEQ_BATCH))
    return (block_out, grad_cur, grad_kernel, grad_gain)


def solution(mesh):
    split = Mesh(
        mesh.devices.reshape(8, 2, 8, 2, 2), ("seq_0", "seq_1", "seq_2", "batch_0", "batch_1")
    )
    placed = (
        P(BATCH, SEQ, None),
        P(BATCH, SEQ, None),
        P(SEQ, None),
        P(SEQ, None),
        P(),
        P(),
        P(BATCH, SEQ, None),
    )
    return jax.shard_map(
        on_device,
        mesh=split,
        in_specs=placed,
        out_specs=(P(BATCH, SEQ, None), P(BATCH, SEQ, None), P(), P()),
        check_vma=False,
    )
```

profile of v0, /device:TPU:1, one launch (start us, length us, event | category | flops | bytes accessed | tf_op | source)
XLA Modules:
  0.0 339.7 jit_solution(5236102935190227426)
XLA Ops:
  7.2 0.0 copy-start
  7.2 0.0 copy-start.3
  7.2 0.0 all-gather.9.cloned.1.call-start
  7.2 4.6 %all-gather.3 = bf16[2,12,1536]{2,1,0:T(8,128)(2,1)S(1)} all-gather(bf16[1,12,1536]{2,1,0:T(8,128)(2,1)} %bitcast.20), channel_id=3, replica_groups=mesh['seq_0'=8,'seq_1'=2,'seq_2'=8,'batch_0'=2,'batch_1'=2] {'seq_1'}, dimensions={0}, use_global_device_ids=true | all-gather | bytes 110592 | tf_op jit(solution)/shard_map/all_gather | solution.py:24
  11.8 27.5 %all_gather.22 = bf16[16,12,1536]{2,1,0:T(8,128)(2,1)S(1)} all-gather(bf16[2,12,1536]{2,1,0:T(8,128)(2,1)S(1)} %all-gather.3), channel_id=1, replica_groups=mesh['seq_0'=8,'seq_1'=2,'seq_2'=8,'batch_0'=2,'batch_1'=2] {'seq_0'}, dimensions={0}, use_global_device_ids=true | all-gather | bytes 663552 | tf_op jit(solution)/shard_map/all_gather | solution.py:24
  39.3 1.1 copy.17
  40.4 0.0 all-gather.9.cloned.1.call-update
  40.5 0.0 copy-start.15
  40.5 0.0 copy-start.1
  40.5 0.0 all-gather.7.cloned.1.call-start
  40.5 0.0 copy-done.3
  40.5 4.0 %all-gather.2 = bf16[2,12,1536]{2,1,0:T(8,128)(2,1)S(1)} all-gather(bf16[1,12,1536]{2,1,0:T(8,128)(2,1)S(1)} %bitcast.21), channel_id=2, replica_groups=mesh['seq_0'=8,'seq_1'=2,'seq_2'=8,'batch_0'=2,'batch_1'=2] {'seq_1'}, dimensions={0}, use_global_device_ids=true | all-gather | bytes 110592 | tf_op jit(solution)/shard_map/all_gather | solution.py:24
  44.5 20.5 %all_gather.19 = bf16[16,12,1536]{2,1,0:T(8,128)(2,1)S(1)} all-gather(bf16[2,12,1536]{2,1,0:T(8,128)(2,1)S(1)} %all-gather.2), channel_id=1, replica_groups=mesh['seq_0'=8,'seq_1'=2,'seq_2'=8,'batch_0'=2,'batch_1'=2] {'seq_0'}, dimensions={0}, use_global_device_ids=true | all-gather | bytes 663552 | tf_op jit(solution)/shard_map/all_gather | solution.py:24
  65.0 1.1 copy.15
  66.2 0.0 all-gather.7.cloned.1.call-update
  66.2 0.0 copy-done.15
  66.2 0.6 slice_reduce_fusion.2
  66.8 0.0 copy-done.1
  66.8 0.1 convert_reduce_fusion
  67.0 0.3 fusion.27
  67.3 0.6 copy-done.22
  67.8 39.6 %all-gather.9.cloned.1.call-done = bf16[128,12,1536]{2,0,1:T(8,128)(2,1)} async-done(((bf16[16,12,1536]{2,0,1:T(8,128)(2,1)}), bf16[128,12,1536]{2,0,1:T(8,128)(2,1)}) %all-gather.9.cloned.1.call-update) | async-done | bytes 4718608 | tf_op jit(solution)/shard_map/all_gather | solution.py:24
  107.5 10.3 %reshape.51 = bf16[8,8,2,12,1536]{4,2,1,0,3:T(2,128)(2,1)} reshape(bf16[128,12,1536]{2,0,1:T(8,128)(2,1)} %all-gather.9.cloned.1.call-done) | data formatting | bytes 9437184 | tf_op jit(solution)/shard_map/reshape | solution.py:26
  117.8 7.7 %copy.21 = bf16[8,8,2,12,1536]{4,3,0,2,1:T(8,128)(2,1)} copy(bf16[8,8,2,12,1536]{4,2,1,0,3:T(2,128)(2,1)} %reshape.51) | data formatting | bytes 9437184 | tf_op jit(solution)/shard_map/reshape | solution.py:26
  125.5 8.2 %reshape.62 = bf16[1536,1536,1]{1,0,2:T(8,128)(2,1)} reshape(bf16[8,2,8,12,1536]{4,3,2,1,0:T(8,128)(2,1)} %bitcast.18) | data formatting | bytes 9437184 | tf_op jit(solution)/shard_map/reshape;reshape | solution.py:18
  133.7 37.0 %all-gather.7.cloned.1.call-done = bf16[128,12,1536]{2,0,1:T(8,128)(2,1)} async-done(((bf16[16,12,1536]{2,0,1:T(8,128)(2,1)}), bf16[128,12,1536]{2,0,1:T(8,128)(2,1)}) %all-gather.7.cloned.1.call-update) | async-done | bytes 4718608 | tf_op jit(solution)/shard_map/all_gather | solution.py:24
  170.7 10.3 %reshape.50 = bf16[8,8,2,12,1536]{4,2,1,0,3:T(2,128)(2,1)} reshape(bf16[128,12,1536]{2,0,1:T(8,128)(2,1)} %all-gather.7.cloned.1.call-done) | data formatting | bytes 9437184 | tf_op jit(solution)/shard_map/reshape | solution.py:26
  181.0 7.7 %copy.22 = bf16[8,8,2,12,1536]{4,3,0,2,1:T(8,128)(2,1)} copy(bf16[8,8,2,12,1536]{4,2,1,0,3:T(2,128)(2,1)} %reshape.50) | data formatting | bytes 9437184 | tf_op jit(solution)/shard_map/reshape | solution.py:26
  188.7 8.2 %reshape.61 = bf16[1536,1536,1]{1,0,2:T(8,128)(2,1)} reshape(bf16[8,2,8,12,1536]{4,3,2,1,0:T(8,128)(2,1)} %bitcast.19) | data formatting | bytes 9437184 | tf_op jit(solution)/shard_map/reshape;reshape | solution.py:18
  196.9 0.0 copy-done.4
  196.9 4.8 %fusion = f32[2,64,1536]{2,1,0:T(8,128)S(1)} fusion(bf16[1536,1536,1]{1,0,2:T(8,128)(2,1)} %reshape.61, bf16[2,64,1536]{2,1,0:T(8,128)(2,1)S(1)} %copy-done.1, f32[1536]{0:T(1024)S(1)} %copy-done.4, f32[2,64]{1,0:T(2,128)S(1)} %fusion.47, f32[2,64]{1,0:T(2,128)S(1)} %broadcast_multiply_fusion), kind=kOutput, calls=%fused_computation.5 | convolution fusion | flops 617938944 | bytes 5905408 | tf_op jit(solution)/shard_map/sbi,io->sbo/dot_general | solution.py:75
  201.7 1.7 broadcast_in_dim.22
  203.4 2.4 convert_element_type.57
  205.8 0.0 copy-done
  205.8 0.0 copy-start.2
  205.8 3.8 %convolution_convert_fusion = bf16[2,128,1536]{2,1,0:T(8,128)(2,1)S(1)} fusion(bf16[2,128,1536]{2,1,0:T(8,128)(2,1)S(1)} %copy-done, bf16[1536,1536,1]{1,0,2:T(8,128)(2,1)} %reshape.62), kind=kOutput, calls=%fused_computation.2 | convolution fusion | flops 1208352768 | bytes 6291456 | tf_op jit(solution)/shard_map/sbo,io->sbi/dot_general | solution.py:92
  209.7 1.3 collective-permute-start.3
  211.0 4.0 %collective-permute-start.2 = (bf16[2,1,1536]{2,1,0:T(2,128)(2,1)S(1)}, bf16[2,1,1536]{2,1,0:T(2,128)(2,1)S(1)}, u32[]{:S(2)}, u32[]{:S(2)}) collective-permute-start(bf16[2,1,1536]{2,1,0:T(2,128)(2,1)S(1)} %get-tuple-element.23), channel_id=1, source_target_pairs={{0,4},{4,8},{8,12},{12,16},{16,20},{20,24},{24,28},{28,32},{32,36}... | collective-permute-start | bytes 18440 | tf_op jit(solution)/shard_map/ppermute | solution.py:43
  215.0 0.2 add_convert_fusion
  215.2 1.3 collective-permute-start.1
  216.5 4.0 %collective-permute-start = (bf16[2,1,1536]{2,1,0:T(2,128)(2,1)S(1)}, bf16[2,1,1536]{2,1,0:T(2,128)(2,1)S(1)}, u32[]{:S(2)}, u32[]{:S(2)}) collective-permute-start(bf16[2,1,1536]{2,1,0:T(2,128)(2,1)S(1)} %get-tuple-element.25), channel_id=1, source_target_pairs={{0,4},{4,8},{8,12},{12,16},{16,20},{20,24},{24,28},{28,32},{32,36}... | collective-permute-start | bytes 18440 | tf_op jit(solution)/shard_map/ppermute | solution.py:43
  220.5 0.0 collective-permute-done.3
  220.5 0.0 collective-permute-done.2
  220.5 0.2 maximum_convert_fusion
  220.8 0.0 collective-permute-done.1
  220.8 0.0 copy-start.16
  220.8 0.5 collective-permute-done
  221.3 0.0 copy-done.7
  221.3 2.8 fusion.4
  224.1 2.2 reshape.52
  226.4 2.8 reduce_sum.83
  229.2 5.7 %fusion.28 = (f32[2,64]{1,0:T(2,128)S(1)}, f32[2,64,1536]{2,1,0:T(8,128)S(1)}) fusion(bf16[2,64,1536]{2,1,0:T(8,128)(2,1)S(1)} %copy-done.1, f32[1536]{0:T(1024)S(1)} %copy-done.4, f32[2,64]{1,0:T(2,128)} %copy-done.13, bf16[2,64,1536]{2,1,0:T(8,128)(2,1)} %reduce_sum.83, bf16[1536,1536,1]{1,0,2:T(8,128)(2,1)} %reshape.61, f32[2,64]{1,0:T(2,128)} %copy-done.20), kind=kOutput, calls=%fused_computation.47 | convolution fusion | flops 619315072 | bytes 6299136 | tf_op jit(solution)/shard_map/sbo,io->sbi/dot_general | solution.py:111
  235.0 0.0 copy-start.17
  235.0 0.4 fusion.26
  235.4 1.0 add_convert_fusion.1
  236.5 0.0 copy-done.6
  236.6 32.7 %all-reduce.1 = (f32[3,1536]{1,0:T(4,128)S(1)}, f32[1536]{0:T(1024)S(1)}) all-reduce(f32[3,1536]{1,0:T(4,128)S(1)} %pad_maximum_fusion.4, f32[1536]{0:T(1024)S(1)} %get-tuple-element.7), channel_id=1, replica_groups=mesh['seq_0'=8,'seq_1'=2,'seq_2'=8,'batch_0'=2,'batch_1'=2] {'seq_0'}, use_global_device_ids=true, to_apply=%region_8.0 | all-reduce | flops 6144 | bytes 49152 | tf_op jit(solution)/shard_map/psum | solution.py:54
  269.2 5.2 %all-reduce.4 = (f32[3,1536]{1,0:T(4,128)S(1)}, f32[1536]{0:T(1024)S(1)}) all-reduce(f32[3,1536]{1,0:T(4,128)S(1)} %get-tuple-element.14, f32[1536]{0:T(1024)S(1)} %get-tuple-element.15), channel_id=1, replica_groups=mesh['seq_0'=8,'seq_1'=2,'seq_2'=8,'batch_0'=2,'batch_1'=2] {'seq_1'}, use_global_device_ids=true, to_apply=%region_9.0 | all-reduce | flops 6144 | bytes 49152 | tf_op jit(solution)/shard_map/psum | solution.py:54
  274.4 20.3 %all-reduce = (f32[3,1536]{1,0:T(4,128)S(1)}, f32[1536]{0:T(1024)S(1)}) all-reduce(f32[3,1536]{1,0:T(4,128)S(1)} %get-tuple-element.20, f32[1536]{0:T(1024)S(1)} %get-tuple-element.21), channel_id=1, replica_groups=mesh['seq_0'=8,'seq_1'=2,'seq_2'=8,'batch_0'=2,'batch_1'=2] {'seq_2'}, use_global_device_ids=true, to_apply=%region_10.0 | all-reduce | flops 6144 | bytes 49152 | tf_op jit(solution)/shard_map/psum | solution.py:54
  294.7 9.0 %all-reduce.3 = (f32[3,1536]{1,0:T(4,128)S(1)}, f32[1536]{0:T(1024)S(1)}) all-reduce(f32[3,1536]{1,0:T(4,128)S(1)} %get-tuple-element.12, f32[1536]{0:T(1024)S(1)} %get-tuple-element.13), channel_id=1, replica_groups=mesh['seq_0'=8,'seq_1'=2,'seq_2'=8,'batch_0'=2,'batch_1'=2] {'batch_0'}, use_global_device_ids=true, to_apply=%region_11.0 | all-reduce | flops 6144 | bytes 49152 | tf_op jit(solution)/shard_map/psum | solution.py:54
  303.7 24.4 %all-reduce.2 = (f32[3,1536]{1,0:T(4,128)}, f32[1536]{0:T(1024)}) all-reduce(f32[3,1536]{1,0:T(4,128)S(1)} %get-tuple-element.18, f32[1536]{0:T(1024)S(1)} %get-tuple-element.19), channel_id=1, replica_groups=mesh['seq_0'=8,'seq_1'=2,'seq_2'=8,'batch_0'=2,'batch_1'=2] {'batch_1'}, use_global_device_ids=true, to_apply=%region_12.0 | all-reduce | flops 6144 | bytes 49152 | tf_op jit(solution)/shard_map/psum | solution.py:54
  328.1 0.0 copy-done.8
  328.1 0.0 copy-done.19
  328.1 4.8 %convolution_convert_fusion.1 = bf16[2,128,1536]{2,1,0:T(8,128)(2,1)} fusion(bf16[1536,1536,1]{1,0,2:T(8,128)(2,1)} %reshape.62, bf16[2,128,1536]{2,1,0:T(8,128)(2,1)S(1)} %add_convert_fusion, bf16[2,1,1536]{2,1,0:T(2,128)(2,1)S(1)} %copy-done.17, bf16[2,1,1536]{2,1,0:T(2,128)(2,1)S(1)} %copy-done.19, f32[1536]{0:T(1024)S(1)} %copy-done.10, ...), kind=kOutput, calls=%fused_computation.3 | convolution fusion | flops 1214251008 | bytes 6322176 | tf_op jit(solution)/shard_map/sbi,io->sbo/dot_general | solution.py:89
  (41 shorter events, 0.2 us)
Async XLA Ops:
  7.2 198.6 %copy-start = (bf16[2,128,1536]{2,1,0:T(8,128)(2,1)S(1)}, bf16[2,128,1536]{2,1,0:T(8,128)(2,1)}, u32[]{:S(2)}) copy-start(bf16[2,128,1536]{2,1,0:T(8,128)(2,1)} %param.13) | copy-start | bytes 2359300
  7.2 33.3 %copy-start.3 = (bf16[12,1536]{1,0:T(8,128)(2,1)S(1)}, bf16[12,1536]{1,0:T(8,128)(2,1)}, u32[]{:S(2)}) copy-start(bf16[12,1536]{1,0:T(8,128)(2,1)} %param.9) | copy-start | bytes 110596
  7.2 100.3 %all-gather.9.cloned.1.call-start = ((), (), s32[]{:S(2)}) async-start(), calls=%async_computation.1 | async-start | bytes 5308416 | tf_op jit(solution)/shard_map/all_gather | solution.py:24
  40.5 25.7 %copy-start.15 = (f32[3,1536]{1,0:T(4,128)S(1)}, f32[3,1536]{1,0:T(4,128)}, u32[]{:S(2)}) copy-start(f32[3,1536]{1,0:T(4,128)} %param.11) | copy-start | bytes 55300
  40.5 26.4 %copy-start.1 = (bf16[2,64,1536]{2,1,0:T(8,128)(2,1)S(1)}, bf16[2,64,1536]{2,1,0:T(8,128)(2,1)}, u32[]{:S(2)}) copy-start(bf16[2,64,1536]{2,1,0:T(8,128)(2,1)} %param.7) | copy-start | bytes 1179652
  40.5 130.2 %all-gather.7.cloned.1.call-start = ((), (), s32[]{:S(2)}) async-start(), calls=%async_computation | async-start | bytes 5308416 | tf_op jit(solution)/shard_map/all_gather | solution.py:24
  67.0 129.9 %copy-start.13 = (f32[2,64]{1,0:T(2,128)}, f32[2,64]{1,0:T(2,128)S(1)}, u32[]{:S(2)}) copy-start(f32[2,64]{1,0:T(2,128)S(1)} %broadcast_multiply_fusion) | copy-start | bytes 1540
  67.3 0.6 copy-start.22
  67.8 129.1 %copy-start.20 = (f32[2,64]{1,0:T(2,128)}, f32[2,64]{1,0:T(2,128)S(1)}, u32[]{:S(2)}) copy-start(f32[2,64]{1,0:T(2,128)S(1)} %fusion.47) | copy-start | bytes 1540
  188.7 8.2 %copy-start.4 = (f32[1536]{0:T(1024)S(1)}, f32[1536]{0:T(1024)}, u32[]{:S(2)}) copy-start(f32[1536]{0:T(1024)} %param.12) | copy-start | bytes 18436
  205.8 9.2 %copy-start.2 = (bf16[2,128,1536]{2,1,0:T(8,128)(2,1)S(1)}, bf16[2,128,1536]{2,1,0:T(8,128)(2,1)}, u32[]{:S(2)}) copy-start(bf16[2,128,1536]{2,1,0:T(8,128)(2,1)} %param.8) | copy-start | bytes 2359300
  209.7 10.9 %collective-permute-start.3 = (bf16[2,1,1536]{2,1,0:T(2,128)(2,1)S(1)}, bf16[2,1,1536]{2,1,0:T(2,128)(2,1)S(1)}, u32[]{:S(2)}, u32[]{:S(2)}) collective-permute-start(bf16[2,1,1536]{2,1,0:T(2,128)(2,1)S(1)} %get-tuple-element.24), channel_id=1, source_target_pairs={{4,0},{8,4},{12,8},{16,12},{20,16},{24,20},{28,24},{32,28},{36,32}... | collective-permute-start | bytes 18440 | tf_op jit(solution)/shard_map/ppermute | solution.py:45
  211.0 9.6 %collective-permute-start.2 = (bf16[2,1,1536]{2,1,0:T(2,128)(2,1)S(1)}, bf16[2,1,1536]{2,1,0:T(2,128)(2,1)S(1)}, u32[]{:S(2)}, u32[]{:S(2)}) collective-permute-start(bf16[2,1,1536]{2,1,0:T(2,128)(2,1)S(1)} %get-tuple-element.23), channel_id=1, source_target_pairs={{0,4},{4,8},{8,12},{12,16},{16,20},{20,24},{24,28},{28,32},{32,36}... | collective-permute-start | bytes 18440 | tf_op jit(solution)/shard_map/ppermute | solution.py:43
  215.2 6.2 %copy-start.7 = (f32[1536]{0:T(1024)S(1)}, f32[1536]{0:T(1024)}, u32[]{:S(2)}) copy-start(f32[1536]{0:T(1024)} %get-tuple-element.9) | copy-start | bytes 18436
  215.2 6.2 %copy-start.9 = (f32[1536]{0:T(1024)S(1)}, f32[1536]{0:T(1024)}, u32[]{:S(2)}) copy-start(f32[1536]{0:T(1024)} %get-tuple-element.10) | copy-start | bytes 18436
  215.2 6.2 %copy-start.11 = (f32[1536]{0:T(1024)S(1)}, f32[1536]{0:T(1024)}, u32[]{:S(2)}) copy-start(f32[1536]{0:T(1024)} %get-tuple-element.11) | copy-start | bytes 18436
  215.2 5.6 %collective-permute-start.1 = (bf16[2,1,1536]{2,1,0:T(2,128)(2,1)S(1)}, bf16[2,1,1536]{2,1,0:T(2,128)(2,1)S(1)}, u32[]{:S(2)}, u32[]{:S(2)}) collective-permute-start(bf16[2,1,1536]{2,1,0:T(2,128)(2,1)S(1)} %get-tuple-element.26), channel_id=1, source_target_pairs={{4,0},{8,4},{12,8},{16,12},{20,16},{24,20},{28,24},{32,28},{36,32}... | collective-permute-start | bytes 18440 | tf_op jit(solution)/shard_map/ppermute | solution.py:45
  216.5 4.8 %collective-permute-start = (bf16[2,1,1536]{2,1,0:T(2,128)(2,1)S(1)}, bf16[2,1,1536]{2,1,0:T(2,128)(2,1)S(1)}, u32[]{:S(2)}, u32[]{:S(2)}) collective-permute-start(bf16[2,1,1536]{2,1,0:T(2,128)(2,1)S(1)} %get-tuple-element.25), channel_id=1, source_target_pairs={{0,4},{4,8},{8,12},{12,16},{16,20},{20,24},{24,28},{28,32},{32,36}... | collective-permute-start | bytes 18440 | tf_op jit(solution)/shard_map/ppermute | solution.py:43
  220.8 3.3 copy-start.16
  221.3 2.8 copy-start.18
  229.2 5.8 %copy-start.23 = (f32[2,64]{1,0:T(2,128)S(1)}, f32[2,64]{1,0:T(2,128)}, u32[]{:S(2)}) copy-start(f32[2,64]{1,0:T(2,128)} %copy-done.22) | copy-start | bytes 1540
  229.2 5.8 %copy-start.14 = (f32[2,64]{1,0:T(2,128)S(1)}, f32[2,64]{1,0:T(2,128)}, u32[]{:S(2)}) copy-start(f32[2,64]{1,0:T(2,128)} %copy-done.13) | copy-start | bytes 1540
  229.2 5.8 %copy-start.21 = (f32[2,64]{1,0:T(2,128)S(1)}, f32[2,64]{1,0:T(2,128)}, u32[]{:S(2)}) copy-start(f32[2,64]{1,0:T(2,128)} %copy-done.20) | copy-start | bytes 1540
  234.9 1.6 copy-start.6
  234.9 1.6 copy-start.5
  234.9 93.1 %copy-start.8 = (f32[1536]{0:T(1024)S(1)}, f32[1536]{0:T(1024)}, u32[]{:S(2)}) copy-start(f32[1536]{0:T(1024)} %get-tuple-element.9) | copy-start | bytes 18436
  234.9 93.1 %copy-start.10 = (f32[1536]{0:T(1024)S(1)}, f32[1536]{0:T(1024)}, u32[]{:S(2)}) copy-start(f32[1536]{0:T(1024)} %get-tuple-element.10) | copy-start | bytes 18436
  234.9 93.1 %copy-start.12 = (f32[1536]{0:T(1024)S(1)}, f32[1536]{0:T(1024)}, u32[]{:S(2)}) copy-start(f32[1536]{0:T(1024)} %get-tuple-element.11) | copy-start | bytes 18436
  235.0 93.1 %copy-start.17 = (bf16[2,1,1536]{2,1,0:T(2,128)(2,1)S(1)}, bf16[2,1,1536]{2,1,0:T(2,128)(2,1)}, u32[]{:S(2)}) copy-start(bf16[2,1,1536]{2,1,0:T(2,128)(2,1)} %copy-done.16) | copy-start | bytes 18436
  235.0 93.1 %copy-start.19 = (bf16[2,1,1536]{2,1,0:T(2,128)(2,1)S(1)}, bf16[2,1,1536]{2,1,0:T(2,128)(2,1)}, u32[]{:S(2)}) copy-start(bf16[2,1,1536]{2,1,0:T(2,128)(2,1)} %copy-done.18) | copy-start | bytes 18436
Sparse Core Ops, SparseCore 0:
  40.6 66.8 all-gather.8
  109.6 61.0 all-gather.6
where the time goes:
time: 341 us; the launch traced here: 340 us
  blocking collectives  148 us (43%)
  waiting for transfers between devices  77.2 us (23%)
  local copies, waits for them, and re-layouts  62.5 us (18%)
  matrix products  19.1 us (6%)
  between operations  14.4 us (4%)
  starting transfers between devices  10.6 us (3%)
  other arithmetic  7.92 us (2%)
    psum x5, blocking collectives, by_axis(): x = lax.psum(x, axis)  91.5 us
    all_gather x2, waiting for transfers between devices, all_blocks(): pieces = lax.all_gather(pieces, axes[k], axis=0, tiled=True)  76.6 us
    all_gather x4, blocking collectives, all_blocks(): pieces = lax.all_gather(pieces, axes[k], axis=0, tiled=True)  56.5 us
    reshape x4, local copies, waits for them, and re-layouts, all_blocks(): pieces = pieces.reshape(*current, *x.shape)  36 us
    another operation x2, local copies, waits for them, and re-layouts, joined_along(): pieces.reshape(*shape[:dim], shape[dim] * shape[dim + 1], *shape[dim + 2:])  16.5 us
    ppermute x2, starting transfers between devices, with_halo(): lax.ppermute(tail, axis, [(i, (i + 1) % count) for i in range(ends)])  7.97 us
  transfers between devices with their start and end apart: 6, of which 3 were waited for; matrix products, arithmetic and copies ran while one was open for 9% of the time, Pallas kernels for 0%

commit v1 on v0

v1 whole, which is shorter than its diff:
```python
import functools
import jax
import jax.numpy as jnp
from jax import lax
from jax.experimental import pallas as pl
from jax.experimental.pallas import tpu as pltpu
from jax.sharding import Mesh
from jax.sharding import PartitionSpec as P

AXES = ("z", "xl", "y", "xh", "core")
F32 = jnp.float32
BF16 = jnp.bfloat16
C = 1536


def remote(src, dst, send, recv, dev):
    return pltpu.make_async_remote_copy(
        src_ref=src, dst_ref=dst, send_sem=send, recv_sem=recv,
        device_id=dev, device_id_type=pl.DeviceIdType.MESH)


def ds128(i, n=128):
    return pl.ds(pl.multiple_of(i, 128), n)


class Here:
    def __init__(self):
        for a in AXES:
            setattr(self, a, lax.axis_index(a))
        self.x = 2 * self.xh + self.xl
        self.quad = self.y // 4
        self.j = self.y % 4

    def on_x(self, step):
        x = (self.x + step + 4) % 4
        return {"xh": x // 2, "xl": x % 2}

    def along(self, core, first, step):
        name = "y" if (core == 0) == first else "z"
        return {name: (getattr(self, name) + step + 8) % 8}


def on_core(here, f):
    for c in (0, 1):
        @pl.when(here.core == c)
        def _(c=c):
            f(c)


def enter(here):
    barrier = pltpu.get_barrier_semaphore()
    peers = []
    for d in range(1, 8):
        peers.append({"y": (here.y + d) % 8})
        peers.append({"z": (here.z + d) % 8})
    for d in range(4):
        for e in range(2):
            if d or e:
                peers.append({**here.on_x(d), "core": (here.core + e) % 2})
    for step in (1, -1):
        for d in range(1, 4):
            peers.append({**here.on_x(step), "y": 4 * here.quad + (here.j + d) % 4})
    seq = here.z * 16 + here.xl * 8 + here.y
    for step in (1, 127):
        n = (seq + step) % 128
        peers.append({"z": n // 16, "xl": n % 16 // 8, "y": n % 8})
    for p in peers:
        pl.semaphore_signal(barrier, inc=1, device_id=p, device_id_type=pl.DeviceIdType.MESH)
    pl.semaphore_wait(barrier, len(peers))


class Weights:
    def __init__(self, here, w, stage, queue, queue0, s0, r0, sx0, rx0, s1, r1, s2, r2, s3, r3, s4, r4):
        self.__dict__.update(locals())

    def block(self, k, t, xl, z, y):
        return self.w.at[k, z, xl, y // 4, :, ds128(512 * t + 128 * (y % 4))]

    def own(self, c, k, cls, step=0):
        h = self.here
        t, xl = (0, c) if cls == 0 else (1 + c, h.xl)
        y, z = (((h.y + step + 8) % 8, h.z) if c == 0 else (h.y, (h.z + step + 8) % 8))
        return self.block(k, t, xl, z, y)

    def chunk(self, c, k, cls, step, other=False):
        h = self.here
        t, xl = (0, c) if cls == 0 else (1 + c, (1 - h.xl) if other else h.xl)
        if c == 0:
            return self.w.at[k, (h.z + step + 8) % 8, xl, :, :, pl.ds(512 * t, 512)]
        y = (h.y + step + 8) % 8
        return self.w.at[k, :, xl, y // 4, :, ds128(512 * t + 128 * (y % 4))]

    def chunks(self, k, n):
        return self.w.at[k, pl.ds(0, n), 0, :, :, pl.ds(0, 512)]

    def pack(self, w_in, w_out):
        h = self.here
        for k, ref in enumerate((w_in, w_out)):
            for j in range(4):
                self.stage[j, k, 12:16, :] = jnp.zeros((4, 256), BF16)
                self.stage[j, k, 0:12, 0:128] = ref[:, 128 * j : 128 * j + 128]
                self.stage[j, k, 0:12, 128:256] = ref[:, ds128(512 * (1 + h.core) + 128 * j)]

    def swap_copies(self):
        h = self.here
        out = []
        for d in range(1, 4):
            j = (h.j + d) % 4
            out.append(remote(self.stage.at[j], self.queue.at[h.j], self.s0.at[d], self.r0.at[d],
                              {"y": 4 * h.quad + j}))
        for d in range(4):
            j = (h.j + d) % 4
            out.append(remote(self.stage.at[j, :, :, pl.ds(0, 128)], self.queue0.at[h.j], self.sx0.at[d],
                              self.rx0.at[d], {**h.on_x(1), "y": 4 * h.quad + j}))
        return out

    def swap_start(self):
        self.queue[self.here.j] = self.stage[self.here.j]
        for c in self.swap_copies():
            c.start()

    def swap_finish(self):
        h = self.here
        for c in self.swap_copies():
            c.wait()
        row = lax.broadcasted_iota(jnp.int32, (48, 64), 0)
        col = lax.broadcasted_iota(jnp.int32, (48, 64), 1)
        pick = ((row // 12 == col // 16) & (row % 12 == col % 16)).astype(BF16)
        for k in (0, 1):
            mine = self.queue[:, k].reshape(64, 256)
            first = jnp.where(h.xl == h.core, mine[:, :128].astype(F32),
                              self.queue0[:, k].reshape(64, 128).astype(F32)).astype(BF16)
            self.w[k, h.z, h.core, h.quad, :, ds128(128 * h.j)] = jnp.dot(
                pick, first, preferred_element_type=F32).astype(BF16)
            self.w[k, h.z, h.xl, h.quad, :, ds128(512 * (1 + h.core) + 128 * h.j)] = jnp.dot(
                pick, mine[:, 128:], preferred_element_type=F32).astype(BF16)

    def first_start(self, c, k):
        for cls in (1, 0):
            for d in (1, 7, 2, 6, 3, 5, 4):
                src = self.own(c, k, cls)
                remote(src, src, self.s1.at[k, cls], self.r1.at[k, cls], self.here.along(c, True, d)).start()

    def seven(self, k):
        return self.w.at[k, pl.ds(0, 7), 0, 0, :, pl.ds(0, 128)]

    def first_wait(self, c, k, cls):
        ref = self.seven(k)
        remote(ref, ref, self.s1.at[k, cls], self.r1.at[k, cls], self.here.along(c, True, 1)).wait_recv()

    def to_core(self, c, k, which, step):
        src = self.chunk(c, k, min(which, 1), step, which == 2)
        remote(src, src, self.s4.at[k, which], self.r4.at[k, which], {"core": 1 - c}).start()

    def hop(self, c, k, cls, step):
        src = self.chunk(c, k, cls, step)
        far = 4 if cls == 1 else 3
        dirs = []
        if step <= 0 and 1 - step <= far:
            dirs.append((1, 1 - step))
        if step >= 0 and 1 + step <= 7 - far:
            dirs.append((-1, 1 + step))
        for way, nth in dirs:
            n = 0 if way == 1 else 1
            remote(src, src, self.s2.at[k, cls, n], self.r2.at[k, cls, n, nth],
                   self.here.along(c, False, way)).start()
        if cls == 1:
            far_x = 1 if step < 0 else -1
            remote(src, src, self.s3.at[k], self.r3.at[k, step % 8], self.here.on_x(far_x)).start()
        self.to_core(c, k, cls, step)

    def second_start(self, c, k):
        for cls in (1, 0):
            self.first_wait(c, k, cls)
            self.hop(c, k, cls, 0)

    def second_step(self, c, k, nth):
        for cls in (1, 0):
            far = 4 if cls == 1 else 3
            for way in (1, -1):
                if nth > (far if way == 1 else 7 - far):
                    continue
                n = 0 if way == 1 else 1
                src = self.chunk(c, k, cls, -nth * way)
                remote(src, src, self.s2.at[k, cls, n], self.r2.at[k, cls, n, nth],
                       self.here.along(c, False, way)).wait_recv()
                self.hop(c, k, cls, -nth * way)
        self.cross_x(c, k, nth - 1)

    def cross_x(self, c, k, nth):
        for step in ((0,) if nth == 0 else (nth, -nth) if nth < 4 else (-4,)):
            src = self.chunk(c, k, 1, step, True)
            remote(src, src, self.s3.at[k], self.r3.at[k, step % 8], self.here.on_x(1)).wait_recv()
            self.to_core(c, k, 2, step)

    def ready(self, c, k):
        ref = self.chunks(k, 8)
        for which in range(3):
            remote(ref, ref, self.s4.at[k, which], self.r4.at[k, which], {"core": 1 - c}).wait_recv()

    def sent(self, c, k):
        h = self.here
        for cls in range(2):
            ref = self.seven(k)
            remote(ref, ref, self.s1.at[k, cls], self.r1.at[k, cls], h.along(c, True, 1)).wait_send()
            far = 4 if cls == 1 else 3
            for n in range(2):
                ref = self.chunks(k, far if n == 0 else 7 - far)
                remote(ref, ref, self.s2.at[k, cls, n], self.r2.at[k, cls, n, 1], h.along(c, False, 1)).wait_send()
        ref = self.chunks(k, 8)
        remote(ref, ref, self.s3.at[k], self.r3.at[k, 0], h.on_x(1)).wait_send()
        for which in range(3):
            remote(ref, ref, self.s4.at[k, which], self.r4.at[k, which], {"core": 1 - c}).wait_send()

    def plan(self):
        return [
            [lambda c: self.first_start(c, 0), lambda c: self.first_start(c, 1)],
            [lambda c: self.second_start(c, 0)],
            [lambda c: self.second_step(c, 0, 1)],
            [lambda c: self.second_step(c, 0, 2), lambda c: self.second_start(c, 1)],
            [lambda c: self.second_step(c, 0, 3), lambda c: self.second_step(c, 1, 1)],
            [lambda c: self.second_step(c, 0, 4), lambda c: self.cross_x(c, 0, 4)],
            [lambda c: self.second_step(c, 1, 2)],
            [lambda c: self.second_step(c, 1, 3)],
            [lambda c: self.second_step(c, 1, 4), lambda c: self.cross_x(c, 1, 4)],
        ]


def weight_scratch():
    sem = pltpu.SemaphoreType.DMA
    return [
        pltpu.VMEM((2, 8, 2, 2, 48, C), BF16),
        pltpu.VMEM((4, 2, 16, 256), BF16),
        pltpu.VMEM((4, 2, 16, 256), BF16),
        pltpu.VMEM((4, 2, 16, 128), BF16),
        sem((4,)), sem((4,)), sem((4,)), sem((4,)),
        sem((2, 2)), sem((2, 2)),
        sem((2, 2, 2)), sem((2, 2, 2, 5)),
        sem((2,)), sem((2, 8)),
        sem((2, 3)), sem((2, 3)),
    ]


EPS = 1e-05
ROWS = 128


class Sum:
    def __init__(self, here, parts, got, send, recv):
        self.__dict__.update(locals())
        self.me = 2 * here.x + here.core

    def group(self, m):
        x = m // 2
        return {"xh": x // 2, "xl": x % 2, "core": m % 2}

    def copies(self, stage):
        h, out = self.here, []
        for d in range(1, 8):
            if stage in (0, 3):
                m = (self.me + d) % 8
                src = self.parts.at[stage, m if stage == 0 else 0]
                dst, to = self.got.at[stage, self.me], self.group(m)
            elif stage == 1:
                src, dst, to = self.parts.at[1, 0], self.got.at[1, h.y], {"y": (h.y + d) % 8}
            else:
                src, dst, to = self.parts.at[2, 0], self.got.at[2, h.z], {"z": (h.z + d) % 8}
            out.append(remote(src, dst, self.send.at[stage, d], self.recv.at[stage, d], to))
        return out

    def mine(self, stage):
        return self.here.y if stage == 1 else self.here.z if stage == 2 else self.me

    def start(self, stage):
        src = self.parts[0, self.me] if stage == 0 else self.parts[stage, 0]
        self.got[stage, self.mine(stage)] = src
        for c in self.copies(stage):
            c.start()

    def finish(self, stage):
        for c in self.copies(stage):
            c.wait()
        if stage < 3:
            total = self.got[stage, 0]
            for n in range(1, 8):
                total = total + self.got[stage, n]
            self.parts[stage + 1, 0] = total


def sum_scratch():
    sem = pltpu.SemaphoreType.DMA
    return [pltpu.VMEM((4, 8, 8, 128), F32), pltpu.VMEM((4, 8, 8, 128), F32), sem((4, 8)), sem((4, 8))]


def picked(rows, cols, where):
    r = lax.broadcasted_iota(jnp.int32, (rows, cols), 0)
    c = lax.broadcasted_iota(jnp.int32, (rows, cols), 1)
    return where(r, c).astype(BF16)


def dot(a, b):
    return jnp.dot(a, b, preferred_element_type=F32)


def dot_t(a, b):
    return lax.dot_general(a, b, (((1,), (1,)), ((), ())), preferred_element_type=F32)


def before(x, first):
    row = lax.broadcasted_iota(jnp.int32, x.shape, 0)
    return jnp.where(row == 0, first, pltpu.roll(x, 1, 0))


def after(x, last):
    row = lax.broadcasted_iota(jnp.int32, x.shape, 0)
    return jnp.where(row == x.shape[0] - 1, last, pltpu.roll(x, x.shape[0] - 1, 0))


def kernel(coarse_hbm, skip_hbm, w_in, w_out, taps, gain, grad_hbm, block_hbm, dx_hbm, gk_out, gg_out, *scratch):
    (ca, sk, go, halo_out, halo_in, act, gp, skp, halo, nrm, dgelu, scale, gm, gc, mer, mix, dn, dx, bo, part,
     in_sem, out_sem, hs, hr) = scratch[:24]
    here = Here()
    w = Weights(here, *scratch[24:40])
    total = Sum(here, *scratch[40:])
    seq = here.z * 16 + here.xl * 8 + here.y

    loads = [pltpu.make_async_copy(a, b, in_sem.at[n])
             for n, (a, b) in enumerate(((coarse_hbm, ca), (skip_hbm, sk), (grad_hbm, go)))]
    for c in loads:
        c.start()
    w.pack(w_out, w_in)
    enter(here)
    w.swap_start()

    for c in loads:
        c.wait()
    row = lax.broadcasted_iota(jnp.int32, (16, C), 0)
    for side in (0, 1):
        rows = jnp.zeros((16, C), F32)
        for n, (ref, last) in enumerate(((ca, 63), (sk, 127), (go, 127))):
            for s in (0, 1):
                if side == 0:
                    r = ref[s, last - 15 : last + 1, :].astype(F32)[15:16]
                else:
                    r = ref[s, 0:16, :].astype(F32)[0:1]
                rows = jnp.where(row == 4 * n + 2 * side + s, r, rows)
        halo_out[side] = rows.astype(BF16)

    def neighbour(step):
        s = (seq + step + 128) % 128
        return {"z": s // 16, "xl": s % 16 // 8, "y": s % 8}

    halos = [remote(halo_out.at[0], halo_in.at[0], hs.at[0], hr.at[0], neighbour(1)),
             remote(halo_out.at[1], halo_in.at[1], hs.at[1], hr.at[1], neighbour(-1))]
    for c in halos:
        c.start()

    w.swap_finish()
    on_core(here, lambda c: w.first_start(c, 0))
    on_core(here, lambda c: w.first_start(c, 1))

    def norm(x):
        x = x.astype(F32)
        centered = x - jnp.mean(x, axis=-1, keepdims=True)
        r = lax.rsqrt(jnp.mean(centered * centered, axis=-1, keepdims=True) + EPS)
        n = centered * r
        u = n * gain[...]
        half = 0.5 + 0.5 * lax.erf(u * 0.7071067811865476)
        return n, r, u, half

    def norm_rows(i):
        at = pl.ds(pl.multiple_of(16 * i, 16), 16)
        n, r, u, half = norm(ca[i // 4, pl.ds(pl.multiple_of(16 * (i % 4), 16), 16), :])
        nrm[at, :] = n
        scale[at, :] = jnp.broadcast_to(r, (16, 128))
        act[at, :] = (u * half).astype(BF16)
        dgelu[at, :] = half + u * (0.3989422804014327 * jnp.exp(-0.5 * u * u))

    lax.fori_loop(0, 4, lambda i, v: (norm_rows(i), v)[1], 0)
    for k in (0, 1):
        on_core(here, lambda c: w.second_start(c, k))
    lax.fori_loop(4, 8, lambda i, v: (norm_rows(i), v)[1], 0)

    for c in halos:
        c.wait()
    left = jnp.where(seq > 0, halo_in[0].astype(F32), 0.0)
    right = jnp.where(seq < 127, halo_in[1].astype(F32), 0.0)
    halo[...] = (left + right).astype(BF16)
    gp[256:272, :] = halo[...]
    on_core(here, lambda c: w.second_step(c, 0, 1))
    on_core(here, lambda c: w.second_step(c, 1, 1))
    _, _, u, half = norm(halo[...])
    act[128:144, :] = (u * half).astype(BF16)
    split = picked(128, 128, lambda r, c: c == 2 * (r % 64) + r // 64)
    for s in (0, 1):
        gp[128 * s : 128 * s + 128, :] = dot(split, go[s]).astype(BF16)
        skp[128 * s : 128 * s + 128, :] = dot(split, sk[s]).astype(BF16)
    on_core(here, lambda c: w.second_step(c, 0, 2))
    on_core(here, lambda c: w.second_step(c, 1, 2))
    on_core(here, lambda c: w.second_step(c, 0, 3))
    on_core(here, lambda c: w.second_step(c, 1, 3))
    on_core(here, lambda c: w.second_step(c, 0, 4))
    on_core(here, lambda c: w.cross_x(c, 0, 4))
    on_core(here, lambda c: w.second_step(c, 1, 4))
    on_core(here, lambda c: w.ready(c, 0))

    def cols(n):
        return ds128(384 * n, 384)

    def back(n):
        at = cols(n)
        rows = w.w[0, pl.ds(2 * n, 2)].reshape(384, C)
        gm[:, at] = dot_t(gp[...], rows).astype(BF16)
        t0, t1, t2 = (taps[t : t + 1, at] for t in range(3))
        edge = gm[256:272, at].astype(F32)
        for s in (0, 1):
            e = gm[128 * s : 128 * s + 64, at].astype(F32)
            o = gm[128 * s + 64 : 128 * s + 128, at].astype(F32)
            e1 = after(e, edge[10 + s : 11 + s])
            o1 = before(o, edge[8 + s : 9 + s])
            gc[64 * s : 64 * s + 64, at] = (t0 * (o + e1) + t1 * (e + o) + t2 * (o1 + e)).astype(BF16)

    lax.fori_loop(0, 2, lambda n, v: (back(n), v)[1], 0)
    on_core(here, lambda c: w.cross_x(c, 1, 4))
    lax.fori_loop(2, 4, lambda n, v: (back(n), v)[1], 0)
    on_core(here, lambda c: w.ready(c, 1))

    def forth(n):
        at = cols(n)
        co = dot(act[...], w.w[1, :, :, :, :, at].reshape(C, 384)).astype(BF16).astype(F32)
        t0, t1, t2 = (taps[t : t + 1, at] for t in range(3))
        skip_edge = halo[:, at].astype(F32)
        sums = [0.0, 0.0, 0.0]
        for s in (0, 1):
            c = co[64 * s : 64 * s + 64]
            me = (c + skp[128 * s : 128 * s + 64, at].astype(F32)).astype(BF16).astype(F32)
            mo = (c + skp[128 * s + 64 : 128 * s + 128, at].astype(F32)).astype(BF16).astype(F32)
            lo = (co[128 + s : 129 + s] + skip_edge[4 + s : 5 + s]).astype(BF16).astype(F32)
            hi = (co[130 + s : 131 + s] + skip_edge[6 + s : 7 + s]).astype(BF16).astype(F32)
            mo1 = before(mo, lo)
            me1 = after(me, hi)
            mix[128 * s : 128 * s + 64, at] = (t0 * mo1 + t1 * me + t2 * mo).astype(BF16)
            mix[128 * s + 64 : 128 * s + 128, at] = (t0 * me + t1 * mo + t2 * me1).astype(BF16)
            e = gm[128 * s : 128 * s + 64, at].astype(F32)
            o = gm[128 * s + 64 : 128 * s + 128, at].astype(F32)
            for t, v in enumerate((mo1 * e + me * o, me * e + mo * o, mo * e + me1 * o)):
                sums[t] = sums[t] + jnp.sum(v, axis=0, keepdims=True)
        for t in range(3):
            part[t : t + 1, at] = sums[t]

    lax.fori_loop(0, 4, lambda n, v: (forth(n), v)[1], 0)

    def gains(n, sums):
        at = cols(n)
        ga = dot_t(gc[...], w.w[1, pl.ds(2 * n, 2)].reshape(384, C))
        gu = ga * dgelu[:, at]
        nn = nrm[:, at]
        part[3:4, at] = jnp.sum(gu * nn, axis=0, keepdims=True)
        d = gu * gain[:, at]
        dn[:, at] = d
        return (sums[0] + jnp.sum(d, axis=1, keepdims=True), sums[1] + jnp.sum(d * nn, axis=1, keepdims=True))

    zero = jnp.zeros((ROWS, 1), F32)
    d_sum, dn_sum = lax.fori_loop(0, 4, gains, (zero, zero))

    for m in range(8):
        for i in range(6):
            total.parts[0, m, i : i + 1, :] = part[m // 2 : m // 2 + 1, 768 * (m % 2) + 128 * i : 768 * (m % 2) + 128 * i + 128]
        total.parts[0, m, 6:8, :] = jnp.zeros((2, 128), F32)
    total.start(0)

    d_mean, dn_mean = d_sum / C, dn_sum / C
    for n in range(4):
        at = pl.ds(384 * n, 384)
        v = scale[:, 0:1] * (dn[:, at] - d_mean - nrm[:, at] * dn_mean)
        dx[:, at] = v.astype(BF16)
    outs = [pltpu.make_async_copy(dx.at[pl.ds(64 * s, 64)], dx_hbm.at[s], out_sem.at[s]) for s in (0, 1)]
    for c in outs:
        c.start()
    total.finish(0)
    total.start(1)
    join = picked(128, 128, lambda r, c: r == 2 * (c % 64) + c // 64)
    for s in (0, 1):
        mer[128 * s : 128 * s + 128, :] = dot(join, mix[128 * s : 128 * s + 128, :]).astype(BF16)

    def final(n):
        at = cols(n)
        bo[:, at] = dot(mer[...], w.w[0, :, :, :, :, at].reshape(C, 384)).astype(BF16)

    lax.fori_loop(0, 2, lambda n, v: (final(n), v)[1], 0)
    total.finish(1)
    total.start(2)
    lax.fori_loop(2, 4, lambda n, v: (final(n), v)[1], 0)
    more = [pltpu.make_async_copy(bo.at[pl.ds(128 * s, 128)], block_hbm.at[s], out_sem.at[2 + s]) for s in (0, 1)]
    for c in more:
        c.start()
    total.finish(2)
    total.start(3)
    for k in (0, 1):
        on_core(here, lambda c: w.sent(c, k))
    for c in outs + more:
        c.wait()
    total.finish(3)
    for m in range(8):
        r, at = m // 2, 768 * (m % 2)
        for i in range(6):
            v = total.got[3, m, i : i + 1, :]
            if r < 3:
                gk_out[r : r + 1, at + 128 * i : at + 128 * i + 128] = v
            else:
                gg_out[0:1, at + 128 * i : at + 128 * i + 128] = v


def on_device(coarse_act, skip_act, proj_in, proj_out, depth_kernel, norm_gain, grad_out):
    vmem = pl.BlockSpec(memory_space=pltpu.VMEM)
    hbm = pl.BlockSpec(memory_space=pl.ANY)
    sem = pltpu.SemaphoreType.DMA

    def b(*shape):
        return pltpu.VMEM(shape, BF16)

    def f(*shape):
        return pltpu.VMEM(shape, F32)

    scratch = [
        b(2, 64, C), b(2, 128, C), b(2, 128, C), b(2, 16, C), b(2, 16, C), b(144, C), b(272, C), b(256, C), b(16, C),
        f(ROWS, C), f(ROWS, C), f(ROWS, 128), b(272, C), b(ROWS, C), b(256, C), b(256, C), f(ROWS, C), b(ROWS, C),
        b(256, C), f(8, C), sem((3,)), sem((4,)), sem((2,)), sem((2,)),
    ] + weight_scratch() + sum_scratch()
    block, dx, gk, gg = pl.pallas_call(
        kernel,
        out_shape=(
            jax.ShapeDtypeStruct((2, 128, C), BF16), jax.ShapeDtypeStruct((2, 64, C), BF16),
            jax.ShapeDtypeStruct((3, C), F32), jax.ShapeDtypeStruct((1, C), F32)),
        in_specs=[hbm, hbm, vmem, vmem, vmem, vmem, hbm],
        out_specs=(hbm, hbm, vmem, vmem),
        scratch_shapes=scratch,
        compiler_params=pltpu.CompilerParams(collective_id=0, has_side_effects=True, vmem_limit_bytes=48 << 20),
        cost_estimate=pl.CostEstimate(flops=3700000000, bytes_accessed=4000000, transcendentals=400000),
    )(coarse_act, skip_act, proj_in, proj_out, depth_kernel, norm_gain.reshape(1, C), grad_out)
    return block, dx, gk, gg.reshape(C)


def solution(mesh):
    split = Mesh(mesh.devices.reshape(8, 2, 8, 2, 2), AXES)
    seq, batch = ("z", "xl", "y"), ("xh", "core")
    big, rows = P(batch, seq, None), P(seq, None)
    return jax.shard_map(
        on_device, mesh=split, in_specs=(big, big, rows, rows, P(), P(), big),
        out_specs=(big, big, P(), P()), check_vma=False)
```

time: 341 us -> 87.6 us (0.26)
  blocking collectives: 148 us -> 0 us
  Pallas kernels: 0 us -> 77.3 us
  waiting for transfers between devices: 77.2 us -> 0 us
  local copies, waits for them, and re-layouts: 62.5 us -> 8.53 us
  matrix products: 19.1 us -> 0 us
  between operations: 14.4 us -> 0.65 us
  starting transfers between devices: 10.6 us -> 0 us
  other arithmetic: 7.92 us -> 0.62 us
    psum x5 -> x0, blocking collectives: 91.5 us -> none  [by_axis(): x = lax.psum(x, axis)]
    pallas_call x0 -> x1, Pallas kernels: none -> 77.3 us  [on_device(): pl.pallas_call(kernel, out_shape=(jax.ShapeDtypeStruct((2, 128, C), BF16)...]
    all_gather x2 -> x0, waiting for transfers between devices: 76.6 us -> none  [all_blocks(): pieces = lax.all_gather(pieces, axes[k], axis=0, tiled=True)]
    all_gather x4 -> x0, blocking collectives: 56.5 us -> none  [all_blocks(): pieces = lax.all_gather(pieces, axes[k], axis=0, tiled=True)]
    reshape x5 -> x1, local copies, waits for them, and re-layouts: 38.2 us -> 0.7 us  [on_device(): norm_gain.reshape(1, C)]
    dot_general x4 -> x0, matrix products: 19.1 us -> none  [the longest x1 5.71 us: on_device(): jnp.einsum('sbo,io->sbi', grad_coarse, whole_in, preferred_element_type=j...]
    another operation x5 -> x0, local copies, waits for them, and re-layouts: 16.5 us -> none  [the longest x2 16.5 us: joined_along(): pieces.reshape(*shape[:dim], shape[dim] * shape[dim + 1], *shape[dim + 2:])]
    ppermute x4 -> x0, starting transfers between devices: 10.6 us -> none  [the longest x2 7.97 us: with_halo(): lax.ppermute(tail, axis, [(i, (i + 1) % count) for i in range(ends)])]
  transfers between devices with their start and end apart: 6 -> 0, of which waited for: 3 -> 0; matrix products, arithmetic and copies ran while one was open for 9% -> 0% of each run, Pallas kernels for 0% -> 0%
where the time goes in v1:
time: 87.6 us; the launch traced here: 87.1 us
  Pallas kernels  77.3 us (88%)
  local copies, waits for them, and re-layouts  8.53 us (10%)
    pallas_call x1, Pallas kernels, on_device(): pl.pallas_call(kernel, out_shape=(jax.ShapeDtypeStruct((2, 128, C), BF16)...  77.3 us
    unnamed x15, local copies, waits for them, and re-layouts  7.82 us

profile of v1, /device:TPU:1, one launch (start us, length us, event | category | flops | bytes accessed | tf_op | source)
XLA Modules:
  0.0 87.1 jit_solution(10451129295474811223)
XLA Ops:
  0.6 0.7 reshape.14.gain
  1.3 0.0 copy-start
  1.3 1.1 %copy-done = bf16[2,128,1536]{2,1,0:T(8,128)(2,1)S(1)} copy-done((bf16[2,128,1536]{2,1,0:T(8,128)(2,1)S(1)}, bf16[2,128,1536]{2,1,0:T(8,128)(2,1)}, u32[]{:S(2)}) %copy-start) | copy-done | bytes 786456
  2.5 0.0 copy-start.1
  2.5 1.1 %copy-done.1 = bf16[2,128,1536]{2,1,0:T(8,128)(2,1)S(1)} copy-done((bf16[2,128,1536]{2,1,0:T(8,128)(2,1)S(1)}, bf16[2,128,1536]{2,1,0:T(8,128)(2,1)}, u32[]{:S(2)}) %copy-start.1) | copy-done | bytes 786456
  3.6 0.0 copy-start.2
  3.6 1.0 %copy-done.2 = bf16[2,64,1536]{2,1,0:T(8,128)(2,1)S(1)} copy-done((bf16[2,64,1536]{2,1,0:T(8,128)(2,1)S(1)}, bf16[2,64,1536]{2,1,0:T(8,128)(2,1)}, u32[]{:S(2)}) %copy-start.2) | copy-done | bytes 393240
  4.6 0.0 copy-start.3
  4.6 0.8 copy-done.3
  5.4 0.0 copy-start.4
  5.4 0.8 copy-done.4
  6.2 0.0 copy-start.5
  6.2 0.7 copy-done.5
  6.9 77.3 %shard_map.102 = (bf16[2,128,1536]{2,1,0:T(8,128)(2,1)S(1)}, bf16[2,64,1536]{2,1,0:T(8,128)(2,1)S(1)}, f32[3,1536]{1,0:T(4,128)S(1)}, f32[1,1536]{1,0:T(1,128)S(1)}) custom-call(bf16[2,64,1536]{2,1,0:T(8,128)(2,1)S(1)} %copy-done.2, bf16[2,128,1536]{2,1,0:T(8,128)(2,1)S(1)} %copy-done, bf16[12,1536]{1,0:T(8,128)(2,1)S(1)} %copy-done.3, ...), custom_call_target="tpu_custom_call" | custom-call | flops 3700000000 | bytes 4000000 | tf_op jit(solution)/shard_map/pallas_call | solution.py:530
  84.3 0.6 reduce
  84.9 0.9 %copy.14 = bf16[2,128,1536]{2,1,0:T(8,128)(2,1)} copy(bf16[2,128,1536]{2,1,0:T(8,128)(2,1)S(1)} %get-tuple-element.16) | data formatting | bytes 1572864
  85.8 0.7 copy.15
  86.5 0.6 copy.16
Async XLA Ops:
  1.3 1.1 %copy-start = (bf16[2,128,1536]{2,1,0:T(8,128)(2,1)S(1)}, bf16[2,128,1536]{2,1,0:T(8,128)(2,1)}, u32[]{:S(2)}) copy-start(bf16[2,128,1536]{2,1,0:T(8,128)(2,1)} %skip_hbm.1) | copy-start | bytes 2359300
  2.5 1.1 %copy-start.1 = (bf16[2,128,1536]{2,1,0:T(8,128)(2,1)S(1)}, bf16[2,128,1536]{2,1,0:T(8,128)(2,1)}, u32[]{:S(2)}) copy-start(bf16[2,128,1536]{2,1,0:T(8,128)(2,1)} %grad_hbm.1) | copy-start | bytes 2359300
  3.6 1.0 %copy-start.2 = (bf16[2,64,1536]{2,1,0:T(8,128)(2,1)S(1)}, bf16[2,64,1536]{2,1,0:T(8,128)(2,1)}, u32[]{:S(2)}) copy-start(bf16[2,64,1536]{2,1,0:T(8,128)(2,1)} %coarse_hbm.1) | copy-start | bytes 1179652
  4.6 0.8 copy-start.3
  5.4 0.8 copy-start.4
  6.2 0.7 copy-start.5

commit v2 on v1

v2 whole, which is shorter than its diff:
```python
import functools
import jax
import jax.numpy as jnp
from jax import lax
from jax.experimental import pallas as pl
from jax.experimental.pallas import tpu as pltpu
from jax.sharding import Mesh
from jax.sharding import PartitionSpec as P

AXES = ("z", "xl", "y", "xh", "core")
F32 = jnp.float32
BF16 = jnp.bfloat16
C = 1536


def remote(src, dst, send, recv, dev):
    return pltpu.make_async_remote_copy(
        src_ref=src, dst_ref=dst, send_sem=send, recv_sem=recv,
        device_id=dev, device_id_type=pl.DeviceIdType.MESH)


def ds128(i, n=128):
    return pl.ds(pl.multiple_of(i, 128), n)


class Here:
    def __init__(self):
        for a in AXES:
            setattr(self, a, lax.axis_index(a))
        self.x = 2 * self.xh + self.xl

    def on_x(self, step):
        x = (self.x + step + 4) % 4
        return {"xh": x // 2, "xl": x % 2}

    def along(self, core, step):
        name = "z" if core == 0 else "y"
        return {name: (getattr(self, name) + step + 8) % 8}


def on_core(here, f):
    for c in (0, 1):
        @pl.when(here.core == c)
        def _(c=c):
            f(c)


def enter(here):
    barrier = pltpu.get_barrier_semaphore()
    peers = []
    for d in range(1, 8):
        peers.append({"y": (here.y + d) % 8})
        peers.append({"z": (here.z + d) % 8})
        for step in (1, -1):
            peers.append({**here.on_x(step), "y": (here.y + d * (1 - here.core)) % 8, "z": (here.z + d * here.core) % 8})
    for d in range(4):
        for e in range(2):
            if d or e:
                peers.append({**here.on_x(d), "core": (here.core + e) % 2})
    seq = here.z * 16 + here.xl * 8 + here.y
    for step in (1, 127):
        n = (seq + step) % 128
        peers.append({"z": n // 16, "xl": n % 16 // 8, "y": n % 8})
    for p in peers:
        pl.semaphore_signal(barrier, inc=1, device_id=p, device_id_type=pl.DeviceIdType.MESH)
    pl.semaphore_wait(barrier, len(peers))


class Weights:
    def __init__(self, here, w, wp, s1, r1, s1x, s2, r2, s3, r3, s4, r4):
        self.__dict__.update(locals())

    def own(self, k, cls):
        h = self.here
        t = 1 + h.core if cls else 0
        return self.wp.at[k, h.z, h.xl, h.y, :, ds128(384 * t, 384)]

    def chunk(self, c, k, cls, step, other=False):
        h = self.here
        t, xl = (0, c) if cls == 0 else (1 + c, (1 - h.xl) if other else h.xl)
        at = pl.ds(384 * t, 384)
        if c == 0:
            return self.wp.at[k, (h.z + step + 8) % 8, xl, :, :, at]
        return self.wp.at[k, :, xl, (h.y + step + 8) % 8, :, at]

    def chunks(self, k, n):
        return self.wp.at[k, pl.ds(0, n), 0, :, :, pl.ds(0, 384)]

    def blocks(self, k, n):
        return self.wp.at[k, pl.ds(0, n), 0, 0, :, pl.ds(0, 384)]

    def pack(self, *refs):
        h = self.here
        for k, ref in enumerate(refs):
            v = ref[...].astype(F32)
            for t in range(3):
                e = v[:, 512 * t + 384 : 512 * t + 512]
                low = jnp.concatenate([e[0:4], e[4:8], e[8:12]], axis=1)
                both = jnp.concatenate([v[:, 512 * t : 512 * t + 384], low], axis=0)
                self.wp[k, h.z, h.xl, h.y, :, 384 * t : 384 * t + 384] = both.astype(BF16)

    def unpack(self, k, t, xl):
        upper = lax.broadcasted_iota(jnp.int32, (8, 384), 0) < 4
        upper1 = upper[:, :128]

        def swapped(v):
            return pltpu.roll(v, 4, 0)

        def unit(i, carry):
            z, q = i // 2, i % 2
            rows, more = [], []
            for p in (0, 1):
                a, b = (self.wp[k, z, xl, 4 * q + 2 * p + n, :, ds128(384 * t, 384)].astype(F32) for n in (0, 1))
                a0, a1, b0, b1 = a[:8], a[8:], b[:8], b[8:]
                rows += [a0, jnp.where(upper, a1, swapped(b0)), swapped(jnp.where(upper, b1, b0))]
                ea, eb = ([v[:, 128 * n : 128 * n + 128] for n in range(3)] for v in (a1, b1))
                more += [jnp.where(upper1, swapped(ea[0]), ea[1]), jnp.where(upper1, swapped(ea[2]), eb[0]),
                         jnp.where(upper1, swapped(eb[1]), eb[2])]
            self.w[k, z, xl, q, :, ds128(512 * t, 384)] = jnp.concatenate(rows, axis=0).astype(BF16)
            self.w[k, z, xl, q, :, ds128(512 * t + 384)] = jnp.concatenate(more, axis=0).astype(BF16)
            return carry

        lax.fori_loop(0, 16, unit, 0)

    def first_start(self, k):
        h = self.here
        src = self.own(k, 1)

        def peer(d):
            return {"y": (h.y + d * (1 - h.core)) % 8, "z": (h.z + d * h.core) % 8}

        order = (4, 3, 5, 2, 6, 1, 7)
        for d in order:
            remote(src, src, self.s1.at[k, 1], self.r1.at[k, 1], peer(d)).start()

        @pl.when(h.xl == h.core)
        def _():
            src = self.own(k, 0)
            for d in order + (0,):
                remote(src, src, self.s1x.at[k], self.r1.at[k, 0], {**h.on_x(1), **peer(d)}).start()
                if d:
                    remote(src, src, self.s1.at[k, 0], self.r1.at[k, 0], peer(d)).start()

    def first_wait(self, c, k, cls):
        h = self.here

        def wait(n):
            ref = self.blocks(k, n)
            remote(ref, ref, self.s1.at[k, cls], self.r1.at[k, cls], {"core": 1 - c}).wait_recv()

        if cls:
            wait(7)
        else:
            pl.when(h.xl == c)(lambda: wait(7))
            pl.when(h.xl != c)(lambda: wait(8))

    def to_core(self, c, k, which, step):
        src = self.chunk(c, k, min(which, 1), step, which == 2)
        remote(src, src, self.s4.at[k, which], self.r4.at[k, which], {"core": 1 - c}).start()

    def hop(self, c, k, cls, step):
        src = self.chunk(c, k, cls, step)
        far = 4 if cls == 1 else 3
        dirs = []
        if step <= 0 and 1 - step <= far:
            dirs.append((1, 1 - step))
        if step >= 0 and 1 + step <= 7 - far:
            dirs.append((-1, 1 + step))
        for way, nth in dirs:
            n = 0 if way == 1 else 1
            remote(src, src, self.s2.at[k, cls, n], self.r2.at[k, cls, n, nth],
                   self.here.along(c, way)).start()
        if cls == 1:
            far_x = (1 if step < 0 else -1) * (-1 if c == 1 and step in (0, -4) else 1)
            remote(src, src, self.s3.at[k], self.r3.at[k, step % 8], self.here.on_x(far_x)).start()
        self.to_core(c, k, cls, step)

    def second_start(self, c, k):
        for cls in (1, 0):
            self.first_wait(c, k, cls)
            self.hop(c, k, cls, 0)

    def second_step(self, c, k, nth):
        for cls in (1, 0):
            far = 4 if cls == 1 else 3
            for way in (1, -1):
                if nth > (far if way == 1 else 7 - far):
                    continue
                n = 0 if way == 1 else 1
                src = self.chunk(c, k, cls, -nth * way)
                remote(src, src, self.s2.at[k, cls, n], self.r2.at[k, cls, n, nth],
                       self.here.along(c, way)).wait_recv()
                self.hop(c, k, cls, -nth * way)
        self.cross_x(c, k, nth - 1)

    def cross_x(self, c, k, nth):
        for step in ((0,) if nth == 0 else (nth, -nth) if nth < 4 else (-4,)):
            src = self.chunk(c, k, 1, step, True)
            remote(src, src, self.s3.at[k], self.r3.at[k, step % 8], self.here.on_x(1)).wait_recv()
            self.to_core(c, k, 2, step)

    def from_core(self, k, which):
        ref = self.chunks(k, 8)
        remote(ref, ref, self.s4.at[k, which], self.r4.at[k, which], {"core": 1 - self.here.core}).wait_recv()

    def sent(self, k):
        h = self.here

        def wait(ref, sem, spare):
            remote(ref, ref, sem, spare, {"core": 1 - h.core}).wait_send()

        wait(self.blocks(k, 7), self.s1.at[k, 1], self.r1.at[k, 1])

        @pl.when(h.xl == h.core)
        def _():
            wait(self.blocks(k, 7), self.s1.at[k, 0], self.r1.at[k, 0])
            wait(self.blocks(k, 8), self.s1x.at[k], self.r1.at[k, 0])

        for cls in range(2):
            far = 4 if cls == 1 else 3
            for n in range(2):
                wait(self.chunks(k, far if n == 0 else 7 - far), self.s2.at[k, cls, n], self.r2.at[k, cls, n, 1])
        wait(self.chunks(k, 8), self.s3.at[k], self.r3.at[k, 0])
        for which in range(3):
            wait(self.chunks(k, 8), self.s4.at[k, which], self.r4.at[k, which])


def weight_scratch():
    sem = pltpu.SemaphoreType.DMA
    return [
        pltpu.VMEM((2, 8, 2, 2, 48, C), BF16),
        pltpu.VMEM((2, 8, 2, 8, 16, 1152), BF16),
        sem((2, 2)), sem((2, 2)), sem((2,)),
        sem((2, 2, 2)), sem((2, 2, 2, 5)),
        sem((2,)), sem((2, 8)),
        sem((2, 3)), sem((2, 3)),
    ]


EPS = 1e-05
ROWS = 128


class Sum:
    def __init__(self, here, parts, got, send, recv):
        self.__dict__.update(locals())
        self.me = 2 * here.x + here.core

    def group(self, m):
        x = m // 2
        return {"xh": x // 2, "xl": x % 2, "core": m % 2}

    def copies(self, stage):
        h, out = self.here, []
        for d in (4, 3, 5, 2, 6, 1, 7):
            if stage in (0, 3):
                m = (self.me + d) % 8
                src = self.parts.at[stage, m if stage == 0 else 0]
                dst, to = self.got.at[stage, self.me], self.group(m)
            elif stage == 1:
                src, dst, to = self.parts.at[1, 0], self.got.at[1, h.y], {"y": (h.y + d) % 8}
            else:
                src, dst, to = self.parts.at[2, 0], self.got.at[2, h.z], {"z": (h.z + d) % 8}
            out.append(remote(src, dst, self.send.at[stage, d], self.recv.at[stage, d], to))
        return out

    def mine(self, stage):
        return self.here.y if stage == 1 else self.here.z if stage == 2 else self.me

    def start(self, stage):
        src = self.parts[0, self.me] if stage == 0 else self.parts[stage, 0]
        self.got[stage, self.mine(stage)] = src
        for c in self.copies(stage):
            c.start()

    def finish(self, stage):
        for c in self.copies(stage):
            c.wait_recv()
        if stage < 3:
            total = self.got[stage, 0]
            for n in range(1, 8):
                total = total + self.got[stage, n]
            self.parts[stage + 1, 0] = total

    def sent(self):
        for stage in range(4):
            for c in self.copies(stage):
                c.wait_send()


def sum_scratch():
    sem = pltpu.SemaphoreType.DMA
    return [pltpu.VMEM((4, 8, 8, 128), F32), pltpu.VMEM((4, 8, 8, 128), F32), sem((4, 8)), sem((4, 8))]


def picked(rows, cols, where):
    r = lax.broadcasted_iota(jnp.int32, (rows, cols), 0)
    c = lax.broadcasted_iota(jnp.int32, (rows, cols), 1)
    return where(r, c).astype(BF16)


def dot(a, b):
    return jnp.dot(a, b, preferred_element_type=F32)


def dot_t(a, b):
    return lax.dot_general(a, b, (((1,), (1,)), ((), ())), preferred_element_type=F32)


def before(x, first):
    row = lax.broadcasted_iota(jnp.int32, x.shape, 0)
    return jnp.where(row == 0, first, pltpu.roll(x, 1, 0))


def after(x, last):
    row = lax.broadcasted_iota(jnp.int32, x.shape, 0)
    return jnp.where(row == x.shape[0] - 1, last, pltpu.roll(x, x.shape[0] - 1, 0))


def kernel(coarse_hbm, skip_hbm, w_in, w_out, taps, gain, grad_hbm, block_out, dx_out, gk_out, gg_out, *scratch):
    (ca, sk, go, halo_out, halo_in, act, gp, skp, halo, nrm, dgelu, scale, gm, gc, mer, mix, dn,
     in_sem, hs, hr, gain_row) = scratch[:21]
    gain_row[...] = gain[...].reshape(1, C)
    here = Here()
    w = Weights(here, *scratch[21:32])
    total = Sum(here, *scratch[32:])
    seq = here.z * 16 + here.xl * 8 + here.y

    loads = [pltpu.make_async_copy(a, b, in_sem.at[n])
             for n, (a, b) in enumerate(((coarse_hbm, ca), (skip_hbm, sk), (grad_hbm, go)))]
    for c in loads:
        c.start()
    w.pack(w_out, w_in)
    enter(here)
    w.first_start(0)
    w.first_start(1)
    total.parts[0] = jnp.zeros((8, 8, 128), F32)

    for c in loads:
        c.wait()
    row = lax.broadcasted_iota(jnp.int32, (16, C), 0)
    for side in (0, 1):
        rows = jnp.zeros((16, C), F32)
        for n, (ref, last) in enumerate(((ca, 63), (sk, 127), (go, 127))):
            for s in (0, 1):
                if side == 0:
                    r = ref[s, last - 15 : last + 1, :].astype(F32)[15:16]
                else:
                    r = ref[s, 0:16, :].astype(F32)[0:1]
                rows = jnp.where(row == 4 * n + 2 * side + s, r, rows)
        halo_out[side] = rows.astype(BF16)

    def neighbour(step):
        s = (seq + step + 128) % 128
        return {"z": s // 16, "xl": s % 16 // 8, "y": s % 8}

    halos = [remote(halo_out.at[0], halo_in.at[0], hs.at[0], hr.at[0], neighbour(1)),
             remote(halo_out.at[1], halo_in.at[1], hs.at[1], hr.at[1], neighbour(-1))]
    for c in halos:
        c.start()


    def norm(x):
        x = x.astype(F32)
        centered = x - jnp.mean(x, axis=-1, keepdims=True)
        r = lax.rsqrt(jnp.mean(centered * centered, axis=-1, keepdims=True) + EPS)
        n = centered * r
        u = n * gain_row[...]
        half = 0.5 + 0.5 * lax.erf(u * 0.7071067811865476)
        return n, r, u, half

    def norm_rows(i):
        at = pl.ds(pl.multiple_of(16 * i, 16), 16)
        n, r, u, half = norm(ca[i // 4, pl.ds(pl.multiple_of(16 * (i % 4), 16), 16), :])
        nrm[at, :] = n
        scale[at, :] = jnp.broadcast_to(r, (16, 128))
        act[at, :] = (u * half).astype(BF16)
        dgelu[at, :] = half + u * (0.3989422804014327 * jnp.exp(-0.5 * u * u))

    lax.fori_loop(0, 4, lambda i, v: (norm_rows(i), v)[1], 0)
    for k in (0, 1):
        on_core(here, lambda c: w.second_start(c, k))
    lax.fori_loop(4, 8, lambda i, v: (norm_rows(i), v)[1], 0)

    for c in halos:
        c.wait_recv()
    left = jnp.where(seq > 0, halo_in[0].astype(F32), 0.0)
    right = jnp.where(seq < 127, halo_in[1].astype(F32), 0.0)
    halo[...] = (left + right).astype(BF16)
    gp[256:272, :] = halo[...]
    on_core(here, lambda c: w.second_step(c, 0, 1))
    on_core(here, lambda c: w.second_step(c, 1, 1))
    _, _, u, half = norm(halo[...])
    act[128:144, :] = (u * half).astype(BF16)
    split = picked(128, 128, lambda r, c: c == 2 * (r % 64) + r // 64)
    for s in (0, 1):
        gp[128 * s : 128 * s + 128, :] = dot(split, go[s]).astype(BF16)
        skp[128 * s : 128 * s + 128, :] = dot(split, sk[s]).astype(BF16)
    for nth in (2, 3, 4):
        for k in (0, 1):
            on_core(here, lambda c: w.second_step(c, k, nth))

    def mine(k):
        w.unpack(k, 1 + here.core, here.xl)
        w.unpack(k, 0, here.core)

    def crossed(k):
        on_core(here, lambda c: w.cross_x(c, k, 4))

    def theirs(k):
        w.unpack(k, 1 + here.core, 1 - here.xl)
        w.from_core(k, 0)
        w.unpack(k, 0, 1 - here.core)
        w.from_core(k, 1)
        w.unpack(k, 2 - here.core, here.xl)

    def last(k):
        w.from_core(k, 2)
        w.unpack(k, 2 - here.core, 1 - here.xl)

    def cols(n):
        return pl.ds(384 * n, 384)

    def back(n):
        at = cols(n)
        rows = w.w[0, pl.ds(2 * n, 2)].reshape(384, C)
        gm[:, at] = dot_t(gp[...], rows).astype(BF16)
        t0, t1, t2 = (taps[t : t + 1, at] for t in range(3))
        edge = gm[256:272, at].astype(F32)
        for s in (0, 1):
            e = gm[128 * s : 128 * s + 64, at].astype(F32)
            o = gm[128 * s + 64 : 128 * s + 128, at].astype(F32)
            e1 = after(e, edge[10 + s : 11 + s])
            o1 = before(o, edge[8 + s : 9 + s])
            gc[64 * s : 64 * s + 64, at] = (t0 * (o + e1) + t1 * (e + o) + t2 * (o1 + e)).astype(BF16)

    mine(0)
    crossed(0)
    mine(1)
    theirs(0)
    crossed(1)
    last(0)
    for n in range(4):
        back(n)
    theirs(1)
    last(1)

    def give(row, n, v):
        for i in range(3):
            m, at = 2 * row + n // 2, 3 * (n % 2) + i
            total.parts[0, m, at : at + 1, :] = v[:, 128 * i : 128 * i + 128]

    def forth(n):
        at = cols(n)
        co = dot(act[...], w.w[1, :, :, :, :, at].reshape(C, 384)).astype(BF16).astype(F32)
        t0, t1, t2 = (taps[t : t + 1, at] for t in range(3))
        skip_edge = halo[:, at].astype(F32)
        sums = [0.0, 0.0, 0.0]
        for s in (0, 1):
            c = co[64 * s : 64 * s + 64]
            me = (c + skp[128 * s : 128 * s + 64, at].astype(F32)).astype(BF16).astype(F32)
            mo = (c + skp[128 * s + 64 : 128 * s + 128, at].astype(F32)).astype(BF16).astype(F32)
            lo = (co[128 + s : 129 + s] + skip_edge[4 + s : 5 + s]).astype(BF16).astype(F32)
            hi = (co[130 + s : 131 + s] + skip_edge[6 + s : 7 + s]).astype(BF16).astype(F32)
            mo1 = before(mo, lo)
            me1 = after(me, hi)
            mix[128 * s : 128 * s + 64, at] = (t0 * mo1 + t1 * me + t2 * mo).astype(BF16)
            mix[128 * s + 64 : 128 * s + 128, at] = (t0 * me + t1 * mo + t2 * me1).astype(BF16)
            e = gm[128 * s : 128 * s + 64, at].astype(F32)
            o = gm[128 * s + 64 : 128 * s + 128, at].astype(F32)
            for t, v in enumerate((mo1 * e + me * o, me * e + mo * o, mo * e + me1 * o)):
                sums[t] = sums[t] + jnp.sum(v, axis=0, keepdims=True)
        for t in range(3):
            give(t, n, sums[t])

    for n in range(4):
        forth(n)

    def gains(n, sums):
        at = cols(n)
        ga = dot_t(gc[...], w.w[1, pl.ds(2 * n, 2)].reshape(384, C))
        gu = ga * dgelu[:, at]
        nn = nrm[:, at]
        give(3, n, jnp.sum(gu * nn, axis=0, keepdims=True))
        d = gu * gain_row[:, at]
        dn[:, at] = d
        return (sums[0] + jnp.sum(d, axis=1, keepdims=True), sums[1] + jnp.sum(d * nn, axis=1, keepdims=True))

    sums = (0.0, 0.0)
    for n in range(4):
        sums = gains(n, sums)
    d_sum, dn_sum = sums

    total.start(0)

    d_mean, dn_mean = d_sum / C, dn_sum / C
    for n in range(4):
        at = pl.ds(384 * n, 384)
        v = scale[:, 0:1] * (dn[:, at] - d_mean - nrm[:, at] * dn_mean)
        for s in (0, 1):
            dx_out[s, :, at] = v[64 * s : 64 * s + 64].astype(BF16)
    total.finish(0)
    total.start(1)
    join = picked(128, 128, lambda r, c: r == 2 * (c % 64) + c // 64)
    for s in (0, 1):
        mer[128 * s : 128 * s + 128, :] = dot(join, mix[128 * s : 128 * s + 128, :]).astype(BF16)

    def final(n):
        at = cols(n)
        v = dot(mer[...], w.w[0, :, :, :, :, at].reshape(C, 384)).astype(BF16)
        for s in (0, 1):
            block_out[s, :, at] = v[128 * s : 128 * s + 128]

    final(0)
    final(1)
    total.finish(1)
    total.start(2)
    final(2)
    final(3)
    total.finish(2)
    total.start(3)
    for k in (0, 1):
        w.sent(k)
    for c in halos:
        c.wait_send()
    total.finish(3)
    total.sent()
    for m in range(8):
        r, at = m // 2, 768 * (m % 2)
        for i in range(6):
            v = total.got[3, m, i : i + 1, :]
            if r < 3:
                gk_out[r : r + 1, at + 128 * i : at + 128 * i + 128] = v
            else:
                gg_out[at + 128 * i : at + 128 * i + 128] = v[0]


def on_device(coarse_act, skip_act, proj_in, proj_out, depth_kernel, norm_gain, grad_out):
    vmem = pl.BlockSpec(memory_space=pltpu.VMEM)
    hbm = pl.BlockSpec(memory_space=pl.ANY)
    sem = pltpu.SemaphoreType.DMA

    def b(*shape):
        return pltpu.VMEM(shape, BF16)

    def f(*shape):
        return pltpu.VMEM(shape, F32)

    scratch = [
        b(2, 64, C), b(2, 128, C), b(2, 128, C), b(2, 16, C), b(2, 16, C), b(144, C), b(272, C), b(256, C), b(16, C),
        f(ROWS, C), f(ROWS, C), f(ROWS, 128), b(272, C), b(ROWS, C), b(256, C), b(256, C), f(ROWS, C),
        sem((3,)), sem((2,)), sem((2,)), f(1, C),
    ] + weight_scratch() + sum_scratch()
    block, dx, gk, gg = pl.pallas_call(
        kernel,
        out_shape=(
            pltpu.VMEM((2, 128, C), BF16), pltpu.VMEM((2, 64, C), BF16), pltpu.VMEM((3, C), F32), pltpu.VMEM((C,), F32)),
        in_specs=[hbm, hbm, vmem, vmem, vmem, vmem, hbm],
        out_specs=(vmem,) * 4,
        scratch_shapes=scratch,
        compiler_params=pltpu.CompilerParams(collective_id=0, has_side_effects=True, vmem_limit_bytes=62 << 20),
        cost_estimate=pl.CostEstimate(flops=3700000000, bytes_accessed=4000000, transcendentals=400000),
    )(coarse_act, skip_act, proj_in, proj_out, depth_kernel, norm_gain, grad_out)
    return hand_over(block, dx, gk, gg)


def hand_over(*arrays):
    def body(*refs):
        sem = refs[8]
        pairs = []
        for n in range(4):
            src, dst = refs[n], refs[4 + n]
            if n < 2:
                half = src.shape[1] // 2
                for s in (0, 1):
                    for q in (0, 1):
                        at = (s, pl.ds(half * q, half))
                        pairs.append((src.at[at], dst.at[at]))
            else:
                pairs.append((src, dst))
        copies = [pltpu.make_async_copy(a, d, sem.at[n]) for n, (a, d) in enumerate(pairs)]
        for c in copies:
            c.start()
        for c in copies:
            c.wait()

    arrays = [pltpu.with_memory_space_constraint(a, pltpu.VMEM) for a in arrays]
    return pl.pallas_call(
        body, out_shape=tuple(jax.ShapeDtypeStruct(s, d) for s, d in (
            ((2, 128, C), BF16), ((2, 64, C), BF16), ((3, C), F32), ((C,), F32))),
        in_specs=[pl.BlockSpec(memory_space=pltpu.VMEM)] * 4, out_specs=(pl.BlockSpec(memory_space=pl.ANY),) * 4,
        scratch_shapes=[pltpu.SemaphoreType.DMA((10,))],
        compiler_params=pltpu.CompilerParams(vmem_limit_bytes=60 << 20),
    )(*arrays)


def solution(mesh):
    split = Mesh(mesh.devices.reshape(8, 2, 8, 2, 2), AXES)
    seq, batch = ("z", "xl", "y"), ("xh", "core")
    big, rows = P(batch, seq, None), P(seq, None)
    return jax.shard_map(
        on_device, mesh=split, in_specs=(big, big, rows, rows, P(), P(), big),
        out_specs=(big, big, P(), P()), check_vma=False)
```

time: 87.6 us -> 74.2 us (0.85)
  local copies, waits for them, and re-layouts: 8.53 us -> 0 us
  Pallas kernels: 77.3 us -> 73.4 us
    unnamed x15 -> x0, local copies, waits for them, and re-layouts: 7.82 us -> none
    pallas_call x1 -> x2, Pallas kernels: 77.3 us -> 73.4 us  [the longest x1 72.3 us: on_device(): pl.pallas_call(kernel, out_shape=(pltpu.VMEM((2, 128, C), BF16), pltpu.VM...]
where the time goes in v2:
time: 74.2 us; the launch traced here: 74 us
  Pallas kernels  73.4 us (99%)
    pallas_call x1, Pallas kernels, on_device(): pl.pallas_call(kernel, out_shape=(pltpu.VMEM((2, 128, C), BF16), pltpu.VM...  72.3 us

profile of v2, /device:TPU:1, one launch (start us, length us, event | category | flops | bytes accessed | tf_op | source)
XLA Modules:
  0.0 74.0 jit_solution(236674131115244017)
XLA Ops:
  0.6 72.3 %shard_map.102 = (bf16[2,128,1536]{2,1,0:T(8,128)(2,1)S(1)}, bf16[2,64,1536]{2,1,0:T(8,128)(2,1)S(1)}, f32[3,1536]{1,0:T(4,128)S(1)}, f32[1536]{0:T(1024)S(1)}) custom-call(bf16[2,64,1536]{2,1,0:T(8,128)(2,1)} %coarse_hbm.1, bf16[2,128,1536]{2,1,0:T(8,128)(2,1)} %skip_hbm.1, bf16[12,1536]{1,0:T(8,128)(2,1)} %w_in.1, bf16[12,1536]{1,0:T(8,128)(2,1)} %w_out.1, ...), custom_call_target="tpu_custom_call" | custom-call | flops 3700000000 | bytes 4000000 | tf_op jit(solution)/shard_map/pallas_call | solution.py:554
  72.9 1.1 %shard_map.103 = (bf16[2,128,1536]{2,1,0:T(8,128)(2,1)}, bf16[2,64,1536]{2,1,0:T(8,128)(2,1)}, f32[3,1536]{1,0:T(4,128)}, f32[1536]{0:T(1024)}) custom-call(bf16[2,128,1536]{2,1,0:T(8,128)(2,1)S(1)} %get-tuple-element.8.refs_0_, bf16[2,64,1536]{2,1,0:T(8,128)(2,1)S(1)} %get-tuple-element.9.refs_1_, f32[3,1536]{1,0:T(4,128)S(1)} %get-tuple-element.10.refs_2_, ...), custom_call_target="tpu_custom_call" | custom-call | tf_op jit(solution)/shard_map/pallas_call | solution.py:588

commit v3 on v2

--- a/solution.py
+++ b/solution.py
@@ -45,7 +45,7 @@
             f(c)
 
 
-def enter(here):
+def greet(here):
     barrier = pltpu.get_barrier_semaphore()
     peers = []
     for d in range(1, 8):
@@ -63,7 +63,7 @@
         peers.append({"z": n // 16, "xl": n % 16 // 8, "y": n % 8})
     for p in peers:
         pl.semaphore_signal(barrier, inc=1, device_id=p, device_id_type=pl.DeviceIdType.MESH)
-    pl.semaphore_wait(barrier, len(peers))
+    return lambda: pl.semaphore_wait(barrier, len(peers))
 
 
 class Weights:
@@ -73,31 +73,37 @@
     def own(self, k, cls):
         h = self.here
         t = 1 + h.core if cls else 0
-        return self.wp.at[k, h.z, h.xl, h.y, :, ds128(384 * t, 384)]
+        return self.wp.at[k, t, h.z, h.xl, h.y]
 
     def chunk(self, c, k, cls, step, other=False):
         h = self.here
         t, xl = (0, c) if cls == 0 else (1 + c, (1 - h.xl) if other else h.xl)
-        at = pl.ds(384 * t, 384)
         if c == 0:
-            return self.wp.at[k, (h.z + step + 8) % 8, xl, :, :, at]
-        return self.wp.at[k, :, xl, (h.y + step + 8) % 8, :, at]
+            return self.wp.at[k, t, (h.z + step + 8) % 8, xl]
+        return self.wp.at[k, t, :, xl, (h.y + step + 8) % 8]
 
     def chunks(self, k, n):
-        return self.wp.at[k, pl.ds(0, n), 0, :, :, pl.ds(0, 384)]
+        return self.wp.at[k, 0, pl.ds(0, n), 0]
 
     def blocks(self, k, n):
-        return self.wp.at[k, pl.ds(0, n), 0, 0, :, pl.ds(0, 384)]
+        return self.wp.at[k, 0, 0, 0, pl.ds(0, n)]
 
     def pack(self, *refs):
         h = self.here
+
+        def one(k, ref, t):
+            v = ref[:, ds128(512 * t, 512)].astype(F32)
+            e = v[:, 384:]
+            low = jnp.concatenate([e[0:4], e[4:8], e[8:12]], axis=1)
+            self.wp[k, t, h.z, h.xl, h.y] = jnp.concatenate([v[:, :384], low], axis=0).astype(BF16)
+
         for k, ref in enumerate(refs):
-            v = ref[...].astype(F32)
-            for t in range(3):
-                e = v[:, 512 * t + 384 : 512 * t + 512]
-                low = jnp.concatenate([e[0:4], e[4:8], e[8:12]], axis=1)
-                both = jnp.concatenate([v[:, 512 * t : 512 * t + 384], low], axis=0)
-                self.wp[k, h.z, h.xl, h.y, :, 384 * t : 384 * t + 384] = both.astype(BF16)
+            one(k, ref, 1 + h.core)
+
+        @pl.when(h.xl == h.core)
+        def _():
+            for k, ref in enumerate(refs):
+                one(k, ref, 0)
 
     def unpack(self, k, t, xl):
         upper = lax.broadcasted_iota(jnp.int32, (8, 384), 0) < 4
@@ -110,36 +116,41 @@
             z, q = i // 2, i % 2
             rows, more = [], []
             for p in (0, 1):
-                a, b = (self.wp[k, z, xl, 4 * q + 2 * p + n, :, ds128(384 * t, 384)].astype(F32) for n in (0, 1))
+                a, b = (self.wp[k, t, z, xl, 4 * q + 2 * p + n].astype(F32) for n in (0, 1))
                 a0, a1, b0, b1 = a[:8], a[8:], b[:8], b[8:]
                 rows += [a0, jnp.where(upper, a1, swapped(b0)), swapped(jnp.where(upper, b1, b0))]
                 ea, eb = ([v[:, 128 * n : 128 * n + 128] for n in range(3)] for v in (a1, b1))
                 more += [jnp.where(upper1, swapped(ea[0]), ea[1]), jnp.where(upper1, swapped(ea[2]), eb[0]),
                          jnp.where(upper1, swapped(eb[1]), eb[2])]
-            self.w[k, z, xl, q, :, ds128(512 * t, 384)] = jnp.concatenate(rows, axis=0).astype(BF16)
-            self.w[k, z, xl, q, :, ds128(512 * t + 384)] = jnp.concatenate(more, axis=0).astype(BF16)
+            at = pl.ds(pl.multiple_of(192 * z + 96 * xl + 48 * q, 16), 48)
+            self.w[k, at, ds128(512 * t, 384)] = jnp.concatenate(rows, axis=0).astype(BF16)
+            self.w[k, at, ds128(512 * t + 384)] = jnp.concatenate(more, axis=0).astype(BF16)
             return carry
 
-        lax.fori_loop(0, 16, unit, 0)
-
-    def first_start(self, k):
+        lax.fori_loop(0, 16, unit, 0, unroll=4)
+
+    def first_start(self, k, cls):
         h = self.here
-        src = self.own(k, 1)
+        src = self.own(k, cls)
 
         def peer(d):
             return {"y": (h.y + d * (1 - h.core)) % 8, "z": (h.z + d * h.core) % 8}
 
+        def send(d):
+            remote(src, src, self.s1.at[k, cls], self.r1.at[k, cls], peer(d)).start()
+
         order = (4, 3, 5, 2, 6, 1, 7)
-        for d in order:
-            remote(src, src, self.s1.at[k, 1], self.r1.at[k, 1], peer(d)).start()
+        if cls:
+            for d in order:
+                send(d)
+            return
 
         @pl.when(h.xl == h.core)
         def _():
-            src = self.own(k, 0)
             for d in order + (0,):
                 remote(src, src, self.s1x.at[k], self.r1.at[k, 0], {**h.on_x(1), **peer(d)}).start()
                 if d:
-                    remote(src, src, self.s1.at[k, 0], self.r1.at[k, 0], peer(d)).start()
+                    send(d)
 
     def first_wait(self, c, k, cls):
         h = self.here
@@ -175,23 +186,22 @@
             remote(src, src, self.s3.at[k], self.r3.at[k, step % 8], self.here.on_x(far_x)).start()
         self.to_core(c, k, cls, step)
 
-    def second_start(self, c, k):
-        for cls in (1, 0):
+    def second_step(self, c, k, cls, nth):
+        if nth == 0:
             self.first_wait(c, k, cls)
             self.hop(c, k, cls, 0)
-
-    def second_step(self, c, k, nth):
-        for cls in (1, 0):
-            far = 4 if cls == 1 else 3
-            for way in (1, -1):
-                if nth > (far if way == 1 else 7 - far):
-                    continue
-                n = 0 if way == 1 else 1
-                src = self.chunk(c, k, cls, -nth * way)
-                remote(src, src, self.s2.at[k, cls, n], self.r2.at[k, cls, n, nth],
-                       self.here.along(c, way)).wait_recv()
-                self.hop(c, k, cls, -nth * way)
-        self.cross_x(c, k, nth - 1)
+            return
+        far = 4 if cls == 1 else 3
+        for way in (1, -1):
+            if nth > (far if way == 1 else 7 - far):
+                continue
+            n = 0 if way == 1 else 1
+            src = self.chunk(c, k, cls, -nth * way)
+            remote(src, src, self.s2.at[k, cls, n], self.r2.at[k, cls, n, nth],
+                   self.here.along(c, way)).wait_recv()
+            self.hop(c, k, cls, -nth * way)
+        if cls:
+            self.cross_x(c, k, nth - 1)
 
     def cross_x(self, c, k, nth):
         for step in ((0,) if nth == 0 else (nth, -nth) if nth < 4 else (-4,)):
@@ -228,8 +238,8 @@
 def weight_scratch():
     sem = pltpu.SemaphoreType.DMA
     return [
-        pltpu.VMEM((2, 8, 2, 2, 48, C), BF16),
-        pltpu.VMEM((2, 8, 2, 8, 16, 1152), BF16),
+        pltpu.VMEM((2, C, C), BF16),
+        pltpu.VMEM((2, 3, 8, 2, 8, 16, 384), BF16),
         sem((2, 2)), sem((2, 2)), sem((2,)),
         sem((2, 2, 2)), sem((2, 2, 2, 5)),
         sem((2,)), sem((2, 8)),
@@ -282,8 +292,8 @@
                 total = total + self.got[stage, n]
             self.parts[stage + 1, 0] = total
 
-    def sent(self):
-        for stage in range(4):
+    def sent(self, *stages):
+        for stage in stages:
             for c in self.copies(stage):
                 c.wait_send()
 
@@ -317,27 +327,35 @@
     return jnp.where(row == x.shape[0] - 1, last, pltpu.roll(x, x.shape[0] - 1, 0))
 
 
-def kernel(coarse_hbm, skip_hbm, w_in, w_out, taps, gain, grad_hbm, block_out, dx_out, gk_out, gg_out, *scratch):
+def kernel(coarse_hbm, skip_hbm, in_hbm, out_hbm, taps_hbm, gain_hbm, grad_hbm, block_out, dx_out, gk_out, gg_out, *scratch):
     (ca, sk, go, halo_out, halo_in, act, gp, skp, halo, nrm, dgelu, scale, gm, gc, mer, mix, dn,
-     in_sem, hs, hr, gain_row) = scratch[:21]
-    gain_row[...] = gain[...].reshape(1, C)
+     in_sem, hs, hr, gain_row, w_in, w_out, taps, gain) = scratch[:25]
     here = Here()
-    w = Weights(here, *scratch[21:32])
-    total = Sum(here, *scratch[32:])
+    w = Weights(here, *scratch[25:36])
+    total = Sum(here, *scratch[36:])
     seq = here.z * 16 + here.xl * 8 + here.y
 
-    loads = [pltpu.make_async_copy(a, b, in_sem.at[n])
-             for n, (a, b) in enumerate(((coarse_hbm, ca), (skip_hbm, sk), (grad_hbm, go)))]
+    loads = [pltpu.make_async_copy(a, b, in_sem.at[n]) for n, (a, b) in enumerate((
+        (out_hbm, w_out), (in_hbm, w_in), (coarse_hbm, ca), (skip_hbm, sk), (grad_hbm, go), (taps_hbm, taps),
+        (gain_hbm, gain)))]
     for c in loads:
         c.start()
+    all_here = greet(here)
+    for c in loads[:2]:
+        c.wait()
     w.pack(w_out, w_in)
-    enter(here)
-    w.first_start(0)
-    w.first_start(1)
+    all_here()
+    for cls, k in ((1, 0), (0, 0), (1, 1), (0, 1)):
+        w.first_start(k, cls)
     total.parts[0] = jnp.zeros((8, 8, 128), F32)
 
-    for c in loads:
+    def ring(*steps):
+        for cls, k, nth in steps:
+            on_core(here, lambda c: w.second_step(c, k, cls, nth))
+
+    for c in loads[2:]:
         c.wait()
+    gain_row[...] = gain[...].reshape(1, C)
     row = lax.broadcasted_iota(jnp.int32, (16, C), 0)
     for side in (0, 1):
         rows = jnp.zeros((16, C), F32)
@@ -378,8 +396,7 @@
         dgelu[at, :] = half + u * (0.3989422804014327 * jnp.exp(-0.5 * u * u))
 
     lax.fori_loop(0, 4, lambda i, v: (norm_rows(i), v)[1], 0)
-    for k in (0, 1):
-        on_core(here, lambda c: w.second_start(c, k))
+    ring((1, 0, 0), (0, 0, 0), (1, 1, 0), (0, 1, 0))
     lax.fori_loop(4, 8, lambda i, v: (norm_rows(i), v)[1], 0)
 
     for c in halos:
@@ -388,21 +405,16 @@
     right = jnp.where(seq < 127, halo_in[1].astype(F32), 0.0)
     halo[...] = (left + right).astype(BF16)
     gp[256:272, :] = halo[...]
-    on_core(here, lambda c: w.second_step(c, 0, 1))
-    on_core(here, lambda c: w.second_step(c, 1, 1))
+    ring((1, 0, 1), (0, 0, 1), (1, 1, 1), (0, 1, 1))
     _, _, u, half = norm(halo[...])
     act[128:144, :] = (u * half).astype(BF16)
     split = picked(128, 128, lambda r, c: c == 2 * (r % 64) + r // 64)
     for s in (0, 1):
         gp[128 * s : 128 * s + 128, :] = dot(split, go[s]).astype(BF16)
         skp[128 * s : 128 * s + 128, :] = dot(split, sk[s]).astype(BF16)
-    for nth in (2, 3, 4):
-        for k in (0, 1):
-            on_core(here, lambda c: w.second_step(c, k, nth))
-
-    def mine(k):
-        w.unpack(k, 1 + here.core, here.xl)
-        w.unpack(k, 0, here.core)
+    for nth in (2, 3):
+        ring((1, 0, nth), (0, 0, nth), (1, 1, nth), (0, 1, nth))
+    ring((1, 0, 4), (0, 0, 4), (1, 1, 4), (0, 1, 4))
 
     def crossed(k):
         on_core(here, lambda c: w.cross_x(c, k, 4))
@@ -419,11 +431,11 @@
         w.unpack(k, 2 - here.core, 1 - here.xl)
 
     def cols(n):
-        return pl.ds(384 * n, 384)
+        return pl.ds(512 * n, 512)
 
     def back(n):
         at = cols(n)
-        rows = w.w[0, pl.ds(2 * n, 2)].reshape(384, C)
+        rows = w.w[0, cols(n), :]
         gm[:, at] = dot_t(gp[...], rows).astype(BF16)
         t0, t1, t2 = (taps[t : t + 1, at] for t in range(3))
         edge = gm[256:272, at].astype(F32)
@@ -434,25 +446,28 @@
             o1 = before(o, edge[8 + s : 9 + s])
             gc[64 * s : 64 * s + 64, at] = (t0 * (o + e1) + t1 * (e + o) + t2 * (o1 + e)).astype(BF16)
 
-    mine(0)
+    w.unpack(0, 1 + here.core, here.xl)
+    w.unpack(0, 0, here.core)
     crossed(0)
-    mine(1)
+    w.unpack(1, 1 + here.core, here.xl)
+    w.unpack(1, 0, here.core)
     theirs(0)
+    last(0)
+    back(0)
     crossed(1)
-    last(0)
-    for n in range(4):
-        back(n)
+    back(1)
+    back(2)
     theirs(1)
     last(1)
 
     def give(row, n, v):
-        for i in range(3):
-            m, at = 2 * row + n // 2, 3 * (n % 2) + i
+        for i in range(4):
+            m, at = (12 * row + 4 * n + i) // 6, (12 * row + 4 * n + i) % 6
             total.parts[0, m, at : at + 1, :] = v[:, 128 * i : 128 * i + 128]
 
     def forth(n):
         at = cols(n)
-        co = dot(act[...], w.w[1, :, :, :, :, at].reshape(C, 384)).astype(BF16).astype(F32)
+        co = dot(act[...], w.w[1, :, at]).astype(BF16).astype(F32)
         t0, t1, t2 = (taps[t : t + 1, at] for t in range(3))
         skip_edge = halo[:, at].astype(F32)
         sums = [0.0, 0.0, 0.0]
@@ -473,12 +488,12 @@
         for t in range(3):
             give(t, n, sums[t])
 
-    for n in range(4):
+    for n in range(3):
         forth(n)
 
     def gains(n, sums):
         at = cols(n)
-        ga = dot_t(gc[...], w.w[1, pl.ds(2 * n, 2)].reshape(384, C))
+        ga = dot_t(gc[...], w.w[1, at, :])
         gu = ga * dgelu[:, at]
         nn = nrm[:, at]
         give(3, n, jnp.sum(gu * nn, axis=0, keepdims=True))
@@ -487,15 +502,15 @@
         return (sums[0] + jnp.sum(d, axis=1, keepdims=True), sums[1] + jnp.sum(d * nn, axis=1, keepdims=True))
 
     sums = (0.0, 0.0)
-    for n in range(4):
+    for n in range(3):
         sums = gains(n, sums)
     d_sum, dn_sum = sums
 
     total.start(0)
 
     d_mean, dn_mean = d_sum / C, dn_sum / C
-    for n in range(4):
-        at = pl.ds(384 * n, 384)
+    for n in range(3):
+        at = cols(n)
         v = scale[:, 0:1] * (dn[:, at] - d_mean - nrm[:, at] * dn_mean)
         for s in (0, 1):
             dx_out[s, :, at] = v[64 * s : 64 * s + 64].astype(BF16)
@@ -507,24 +522,24 @@
 
     def final(n):
         at = cols(n)
-        v = dot(mer[...], w.w[0, :, :, :, :, at].reshape(C, 384)).astype(BF16)
+        v = dot(mer[...], w.w[0, :, at]).astype(BF16)
         for s in (0, 1):
             block_out[s, :, at] = v[128 * s : 128 * s + 128]
 
     final(0)
-    final(1)
     total.finish(1)
     total.start(2)
+    final(1)
     final(2)
-    final(3)
     total.finish(2)
     total.start(3)
     for k in (0, 1):
         w.sent(k)
     for c in halos:
         c.wait_send()
+    total.sent(0, 1, 2)
     total.finish(3)
-    total.sent()
+    total.sent(3)
     for m in range(8):
         r, at = m // 2, 768 * (m % 2)
         for i in range(6):
@@ -549,13 +564,13 @@
     scratch = [
         b(2, 64, C), b(2, 128, C), b(2, 128, C), b(2, 16, C), b(2, 16, C), b(144, C), b(272, C), b(256, C), b(16, C),
         f(ROWS, C), f(ROWS, C), f(ROWS, 128), b(272, C), b(ROWS, C), b(256, C), b(256, C), f(ROWS, C),
-        sem((3,)), sem((2,)), sem((2,)), f(1, C),
+        sem((7,)), sem((2,)), sem((2,)), f(1, C), b(12, C), b(12, C), f(3, C), f(C),
     ] + weight_scratch() + sum_scratch()
     block, dx, gk, gg = pl.pallas_call(
         kernel,
         out_shape=(
             pltpu.VMEM((2, 128, C), BF16), pltpu.VMEM((2, 64, C), BF16), pltpu.VMEM((3, C), F32), pltpu.VMEM((C,), F32)),
-        in_specs=[hbm, hbm, vmem, vmem, vmem, vmem, hbm],
+        in_specs=[hbm] * 7,
         out_specs=(vmem,) * 4,
         scratch_shapes=scratch,
         compiler_params=pltpu.CompilerParams(collective_id=0, has_side_effects=True, vmem_limit_bytes=62 << 20),

time: 74.2 us -> 71.8 us (0.968)
  Pallas kernels: 73.4 us -> 71 us
    pallas_call x1, Pallas kernels: 72.3 us -> 69.9 us  [on_device(): pl.pallas_call(kernel, out_shape=(pltpu.VMEM((2, 128, C), BF16), pltpu.VM...]
where the time goes in v3:
time: 71.8 us; the launch traced here: 71.7 us
  Pallas kernels  71 us (99%)
    pallas_call x1, Pallas kernels, on_device(): pl.pallas_call(kernel, out_shape=(pltpu.VMEM((2, 128, C), BF16), pltpu.VM...  69.9 us

profile of v3, /device:TPU:1, one launch (start us, length us, event | category | flops | bytes accessed | tf_op | source)
XLA Modules:
  0.0 71.7 jit_solution(15629256554774374456)
XLA Ops:
  0.6 69.9 %shard_map.102 = (bf16[2,128,1536]{2,1,0:T(8,128)(2,1)S(1)}, bf16[2,64,1536]{2,1,0:T(8,128)(2,1)S(1)}, f32[3,1536]{1,0:T(4,128)S(1)}, f32[1536]{0:T(1024)S(1)}) custom-call(bf16[2,64,1536]{2,1,0:T(8,128)(2,1)} %coarse_hbm.1, bf16[2,128,1536]{2,1,0:T(8,128)(2,1)} %skip_hbm.1, bf16[12,1536]{1,0:T(8,128)(2,1)} %in_hbm.1, bf16[12,1536]{1,0:T(8,128)(2,1)} %out_hbm.1, ...), custom_call_target="tpu_custom_call" | custom-call | flops 3700000000 | bytes 4000000 | tf_op jit(solution)/shard_map/pallas_call | solution.py:569
  70.6 1.1 %shard_map.103 = (bf16[2,128,1536]{2,1,0:T(8,128)(2,1)}, bf16[2,64,1536]{2,1,0:T(8,128)(2,1)}, f32[3,1536]{1,0:T(4,128)}, f32[1536]{0:T(1024)}) custom-call(bf16[2,128,1536]{2,1,0:T(8,128)(2,1)S(1)} %get-tuple-element.8.refs_0_, bf16[2,64,1536]{2,1,0:T(8,128)(2,1)S(1)} %get-tuple-element.9.refs_1_, f32[3,1536]{1,0:T(4,128)S(1)} %get-tuple-element.10.refs_2_, ...), custom_call_target="tpu_custom_call" | custom-call | tf_op jit(solution)/shard_map/pallas_call | solution.py:603
